TPU v7x, 256 devices: a whole 4x4x8 slice. The times are simulated.
256 devices in a mesh: ctx: 64 (over x, y_hi, z), head: 4 (over y_lo, core).
Axes of the slice: x: 4, y: 4 (y_hi: 2, y_lo: 2; y = y_hi * 2 + y_lo), z: 8, core: 2. Of those that a mesh axis runs over, the one named last changes fastest.
Arguments:
- tokens: bfloat16 [8192, 1536], P('ctx', 'head'), may hold values from -6 to 6
- tissue: int32 [8192], P('ctx'), may hold values from 0 to 1, as said below
- conv_taps: float32 [83, 1536], P(None, 'head'), may hold values from -0.625 to 0.625
- conv_bias: float32 [1536], P('head'), may hold values from -3 to 3
- ln_gain: float32 [1536], replicated, may hold values from 0.5 to 2
- w_qkv: bfloat16 [1536, 3, 1024], P(None, None, 'head'), may hold values from -4 to 4
- w_out: bfloat16 [1024, 1536], P('head'), may hold values from -0.75 to 0.75
- drop_seed: int32 [2], replicated, may hold values from 0 to 1048575
- grad_out: bfloat16 [8192, 1536], P('ctx', 'head'), may hold values from -6 to 6
Outputs:
- encoded: bfloat16 [8192, 1536], P('ctx', 'head')
- grad_tokens: bfloat16 [8192, 1536], P('ctx', 'head')
Inputs may be any that keep to these rules, and one draw needn't show every extreme that they name: The tissue tiles of each grid row of 32 columns form one run of columns, and every grid row holds at least one tissue tile. `drop_seed`: element 0 is the dropout seed, element 1 the key counter.
All inputs are finite; a program needn't handle non-finite values.
Results may differ from a plain program's by a relative error of at most 0.039.
Values may be sent and summed in bfloat16 or wider, within the bound.
A program may use at most 128 MiB of HBM per device.

v0:
```python
from functools import partial
import math

import jax
import jax.numpy as jnp
from jax import lax
from jax.sharding import PartitionSpec as P

HEAD_DIM = 64
GRID_COLS = 32


DROP_LEVEL = 103
KEEP_SCALE = 1024.0 / 921.0
NEG = -1e30
EPS = 1e-05


def padded_2(cells, sides, width):
    for axis, dim in sides:
        count = lax.axis_size(axis)
        ends = count - 1
        head = lax.slice_in_dim(cells, 0, width, axis=dim)
        tail = lax.slice_in_dim(cells, cells.shape[dim] - width, cells.shape[dim], axis=dim)
        cells = jnp.concatenate(
            [
                lax.ppermute(tail, axis, [(i, (i + 1) % count) for i in range(ends)]),
                cells,
                lax.ppermute(head, axis, [((i + 1) % count, i) for i in range(ends)]),
            ],
            axis=dim,
        )
    return cells


def keep_mask(anchor, counter, row_ids, col_ids):
    mixed = (
        row_ids * jnp.int32(374761393)
        + col_ids * jnp.int32(668265263)
        + anchor * jnp.int32(1274126177)
        + counter
    )
    mixed = jnp.bitwise_xor(mixed, lax.shift_right_logical(mixed, jnp.full_like(mixed, 15)))
    mixed = mixed * jnp.int32(16777619)
    mixed = jnp.bitwise_xor(mixed, lax.shift_right_logical(mixed, jnp.full_like(mixed, 13)))
    mixed = mixed * jnp.int32(1274126177)
    mixed = jnp.bitwise_xor(mixed, lax.shift_right_logical(mixed, jnp.full_like(mixed, 16)))
    return (jnp.bitwise_and(mixed, jnp.int32(1023)) >= DROP_LEVEL).astype(jnp.float32)


def merged_taps(conv_taps):
    width = conv_taps.shape[1]
    kernel = conv_taps[0:49].reshape(7, 7, width)
    kernel = kernel.at[1:6, 1:6].add(conv_taps[49:74].reshape(5, 5, width))
    return kernel.at[2:5, 2:5].add(conv_taps[74:83].reshape(3, 3, width))


def depthwise(grid, kernel, flipped):
    padded = padded_2(grid, (("ctx", 0),), 3)
    padded = jnp.pad(padded.astype(jnp.float32), ((0, 0), (3, 3), (0, 0)))
    grid_rows, grid_cols = (grid.shape[0], grid.shape[1])
    total = jnp.zeros(grid.shape, jnp.float32)
    for row_off in range(7):
        for col_off in range(7):
            weight = kernel[6 - row_off, 6 - col_off] if flipped else kernel[row_off, col_off]
            total = (
                total
                + weight * padded[row_off : row_off + grid_rows, col_off : col_off + grid_cols]
            )
    return total


def gather_features(value):
    return lax.all_gather(value, "head", axis=1, tiled=True)


def over_keys(step, init, pair, tissue):
    return step(
        init,
        (
            lax.all_gather(pair, "ctx", axis=0, tiled=True),
            lax.all_gather(tissue, "ctx", axis=0, tiled=True),
        ),
        jnp.int32(0),
    )


def softmax_step(query3, scale_factor, state, pieces, start):
    running, totals, values_acc = state
    pair, alive = pieces
    count = pair.shape[0]
    heads = query3.shape[1]
    split = pair.reshape(count, 2, heads, HEAD_DIM)
    scores = (
        jnp.einsum("qhd,khd->hqk", query3, split[:, 0], preferred_element_type=jnp.float32)
        * scale_factor
    )
    usable = (alive > 0)[None, None, :]
    scores = jnp.where(usable, scores, NEG)
    highest = jnp.maximum(running, jnp.max(scores, axis=-1))
    weights = jnp.where(usable, jnp.exp(scores - highest[..., None]), 0.0)
    totals = jnp.sum(weights, axis=-1)
    update = jnp.einsum(
        "hqk,khd->hqd",
        weights.astype(jnp.bfloat16),
        split[:, 1],
        preferred_element_type=jnp.float32,
    )
    return (highest, totals, update)


def query_grad_step(query3, grad3, log_total, shift, scale_factor, state, pieces, start):
    pair, alive = pieces
    count = pair.shape[0]
    heads = query3.shape[1]
    split = pair.reshape(count, 2, heads, HEAD_DIM)
    usable = (alive > 0)[None, None, :]
    scores = (
        jnp.einsum("qhd,khd->hqk", query3, split[:, 0], preferred_element_type=jnp.float32)
        * scale_factor
    )
    probs = jnp.where(usable, jnp.exp(scores - log_total[..., None]), 0.0)
    dprob = jnp.einsum("qhd,khd->hqk", grad3, split[:, 1], preferred_element_type=jnp.float32)
    slope = (probs * (dprob - shift[..., None]) * scale_factor).astype(jnp.bfloat16)
    return jnp.einsum("hqk,khd->qhd", slope, split[:, 0], preferred_element_type=jnp.float32)


def key_grad_step(keys3, values3, tissue, log_all, shift_all, scale_factor, state, piece, start):
    count = piece.shape[0]
    heads = keys3.shape[1]
    split = piece.reshape(count, 2, heads, HEAD_DIM)
    log_rows = log_all.T
    shift_rows = shift_all.T
    usable = (tissue > 0)[None, None, :]
    scores = (
        jnp.einsum("qhd,khd->hqk", split[:, 0], keys3, preferred_element_type=jnp.float32)
        * scale_factor
    )
    probs = jnp.where(usable, jnp.exp(scores - log_rows[..., None]), 0.0)
    dprob = jnp.einsum("qhd,khd->hqk", split[:, 1], values3, preferred_element_type=jnp.float32)
    slope = (probs * (dprob - shift_rows[..., None]) * scale_factor).astype(jnp.bfloat16)
    key_acc = jnp.einsum("hqk,qhd->khd", slope, split[:, 0], preferred_element_type=jnp.float32)
    value_acc = jnp.einsum(
        "hqk,qhd->khd", probs.astype(jnp.bfloat16), split[:, 1], preferred_element_type=jnp.float32
    )
    return (key_acc, value_acc)


def on_device(tokens, tissue, conv_taps, conv_bias, ln_gain, w_qkv, w_out, drop_seed, grad_out):
    rows, width = tokens.shape
    model_width = ln_gain.shape[0]
    heads = w_out.shape[0] // HEAD_DIM
    local_att = heads * HEAD_DIM
    scale_factor = 1.0 / math.sqrt(HEAD_DIM)
    alive_col = tissue.astype(jnp.float32)[:, None]
    kernel = merged_taps(conv_taps)
    grid_shape = (rows // GRID_COLS, GRID_COLS, width)
    masked = tokens * tissue.astype(jnp.bfloat16)[:, None]
    mixed = depthwise(masked.reshape(grid_shape), kernel, False).reshape(rows, width)
    residual = ((masked.astype(jnp.float32) + conv_bias + mixed) * alive_col).astype(jnp.bfloat16)
    stream = gather_features(residual).astype(jnp.float32)
    center = stream - jnp.mean(stream, axis=-1, keepdims=True)
    spread = lax.rsqrt(jnp.mean(center * center, axis=-1, keepdims=True) + EPS)
    unit = center * spread
    normed = (unit * ln_gain).astype(jnp.bfloat16)
    local_w = w_qkv.reshape(model_width, 3 * local_att)
    project = jnp.dot(normed, local_w, preferred_element_type=jnp.float32).astype(jnp.bfloat16)
    project = project.reshape(rows, 3, local_att)
    query3 = project[:, 0].reshape(rows, heads, HEAD_DIM)
    pair = project[:, 1:].reshape(rows, 2 * local_att)
    pair3 = pair.reshape(rows, 2, heads, HEAD_DIM)
    start_state = (
        jnp.full((heads, rows), NEG, jnp.float32),
        jnp.zeros((heads, rows), jnp.float32),
        jnp.zeros((heads, rows, HEAD_DIM), jnp.float32),
    )
    running, totals, values_acc = over_keys(
        partial(softmax_step, query3, scale_factor), start_state, pair, tissue
    )
    attended3 = (values_acc / totals[..., None]).transpose(1, 0, 2).astype(jnp.bfloat16)
    log_total = running + jnp.log(totals)
    partial_out = jnp.dot(
        attended3.reshape(rows, local_att), w_out, preferred_element_type=jnp.float32
    )
    branch = lax.psum_scatter(
        partial_out.astype(jnp.bfloat16), "head", scatter_dimension=1, tiled=True
    ).astype(jnp.float32)
    row_ids = (lax.axis_index("ctx") * rows + lax.iota(jnp.int32, rows))[:, None]
    col_ids = (lax.axis_index("head") * width + lax.iota(jnp.int32, width))[None, :]
    keep = keep_mask(drop_seed[0], drop_seed[1], row_ids, col_ids)
    encoded = ((residual.astype(jnp.float32) + branch * keep * KEEP_SCALE) * alive_col).astype(
        jnp.bfloat16
    )
    upstream = grad_out.astype(jnp.float32) * alive_col
    drop_grad = (upstream * keep * KEEP_SCALE).astype(jnp.bfloat16)
    drop_full = gather_features(drop_grad)
    out_grad = lax.dot_general(
        drop_full, w_out, (((1,), (1,)), ((), ())), preferred_element_type=jnp.float32
    ).astype(jnp.bfloat16)
    grad3 = out_grad.reshape(rows, heads, HEAD_DIM)
    shift = jnp.sum(grad3.astype(jnp.float32) * attended3.astype(jnp.float32), axis=-1).T
    query_grad = over_keys(
        partial(query_grad_step, query3, grad3, log_total, shift, scale_factor),
        jnp.zeros((rows, heads, HEAD_DIM), jnp.float32),
        pair,
        tissue,
    )
    log_all, shift_all = (
        lax.all_gather(log_total.T, "ctx", axis=0, tiled=True),
        lax.all_gather(shift.T, "ctx", axis=0, tiled=True),
    )
    sender = jnp.concatenate([project[:, 0], out_grad], axis=1)
    empty = jnp.zeros((rows, heads, HEAD_DIM), jnp.float32)
    key_step = partial(
        key_grad_step, pair3[:, 0], pair3[:, 1], tissue, log_all, shift_all, scale_factor
    )
    key_acc, value_acc = key_step(
        (empty, empty), lax.all_gather(sender, "ctx", axis=0, tiled=True), jnp.int32(0)
    )
    grads = (
        jnp.stack([query_grad, key_acc, value_acc], axis=1)
        .astype(jnp.bfloat16)
        .reshape(rows, 3 * local_att)
    )
    input_part = lax.dot_general(
        grads, local_w, (((1,), (1,)), ((), ())), preferred_element_type=jnp.float32
    )
    offset = lax.axis_index("head") * width
    normed_grad = lax.psum(input_part.astype(jnp.bfloat16), "head").astype(jnp.float32)
    scaled = normed_grad * ln_gain
    inner = (
        scaled
        - jnp.mean(scaled, axis=-1, keepdims=True)
        - unit * jnp.mean(scaled * unit, axis=-1, keepdims=True)
    )
    layer_grad = lax.dynamic_slice_in_dim(inner * spread, offset, width, 1)
    source_grad = ((upstream + layer_grad) * alive_col).astype(jnp.bfloat16)
    spread_back = depthwise(source_grad.reshape(grid_shape), kernel, True).reshape(rows, width)
    grad_tokens = ((source_grad.astype(jnp.float32) + spread_back) * alive_col).astype(jnp.bfloat16)
    return (encoded, grad_tokens)


def solution(mesh):
    placed = (
        P("ctx", "head"),
        P("ctx"),
        P(None, "head"),
        P("head"),
        P(),
        P(None, None, "head"),
        P("head", None),
        P(),
        P("ctx", "head"),
    )
    return jax.shard_map(
        on_device,
        mesh=mesh,
        in_specs=placed,
        out_specs=(P("ctx", "head"), P("ctx", "head")),
        check_vma=False,
    )
```

profile of v0, /device:TPU:1, one launch (start us, length us, event | category | flops | bytes accessed | tf_op | source)
XLA Modules:
  0.0 753.1 jit_solution(6924447925688933072)
XLA Ops:
  10.1 4.4 collective-permute-start
  20.3 2.8 copy.25
  24.3 1.9 fusion.123
  27.9 7.3 all_gather.24
  35.8 2.3 convolution_convert_fusion.2
  41.4 156.3 %all-gather = s32[64,1,128]{2,1,0:T(1,128)S(1)} all-gather(s32[1,1,128]{2,1,0:T(1,128)} %bitcast.159), channel_id=1, replica_groups=mesh['ctx'=64,'head'=4] {'ctx'}, dimensions={0}, use_global_device_ids=true | all-gather | bytes 33280 | tf_op jit(solution)/shard_map/all_gather | solution.py:82
  199.3 4.5 select_reduce_fusion
  203.8 5.2 fusion
  209.0 5.9 fusion.26
  216.6 2.0 copy.31
  223.4 34.9 %reduce-scatter.4.cloned.1.call-done = bf16[384,128]{1,0:T(8,128)(2,1)} async-done(((bf16[1536,128]{1,0:T(8,128)(2,1)}), bf16[384,128]{1,0:T(8,128)(2,1)}) %reduce-scatter.4.cloned.1.call-update) | async-done | bytes 98320
  260.0 2.5 multiply_convert_fusion.4
  262.5 6.6 all_gather.26
  273.0 155.1 %all_gather.28 = f32[8192,4]{0,1:T(4,128)S(1)} all-gather(f32[128,4]{0,1:T(4,128)S(1)} %bitcast_add_fusion.2), channel_id=1, replica_groups=mesh['ctx'=64,'head'=4] {'ctx'}, dimensions={0}, use_global_device_ids=true | all-gather | bytes 133120 | tf_op jit(solution)/shard_map/all_gather | solution.py:209
  430.6 153.4 %all_gather.29 = f32[8192,4]{0,1:T(4,128)} all-gather(f32[128,4]{0,1:T(4,128)S(1)} %multiply_reduce_fusion.1), channel_id=1, replica_groups=mesh['ctx'=64,'head'=4] {'ctx'}, dimensions={0}, use_global_device_ids=true | all-gather | bytes 133120 | tf_op jit(solution)/shard_map/all_gather | solution.py:210
  584.0 13.8 %fusion.21 = bf16[128,1,4,64]{0,3,2,1:T(8,128)(2,1)} fusion(f32[4,128,8192]{2,1,0:T(8,128)} %copy-done.2, bf16[128,4,64]{0,2,1:T(8,128)(2,1)S(1)} %bitcast.148, f32[4,128]{1,0:T(4,128)S(1)} %bitcast.158, f32[4,128]{1,0:T(4,128)S(1)} %log_add_fusion, pred[8192]{0:T(1024)(128)(4,1)S(1)} %compare_bitcast_fusion, bf16[8192,2,4,64]{0,3,2,1:T(8,128)(2,1)} %bitcast.136), kind=kOutput, calls=%fused_computation.111 | convolution fusion | flops 1103134720 | bytes 25309184 | tf_op jit(solution)/shard_map/hqk,khd->qhd/dot_general | solution.py:125
  597.8 11.3 %copy.30 = bf16[8192,512]{0,1:T(8,128)(2,1)} copy(bf16[8192,512]{1,0:T(8,128)(2,1)} %all-gather.6.cloned.1.call-done) | data formatting | bytes 16777216 | tf_op jit(solution)/shard_map/all_gather | solution.py:218
  609.1 10.7 %exponential_select_fusion = f32[4,8192,128]{2,1,0:T(8,128)} fusion(f32[4,8192]{1,0:T(4,128)S(1)} %bitcast.151, pred[128]{0:T(512)(128)(4,1)S(1)} %broadcast_compare_fusion, bf16[8192,2,4,64]{0,3,2,1:T(8,128)(2,1)} %bitcast.127, bf16[128,2,4,64]{0,3,2,1:T(8,128)(2,1)S(1)} %bitcast.146), kind=kOutput, calls=%fused_computation.1 | convolution fusion | flops 549453824 | bytes 21168640 | tf_op jit(solution)/shard_map/qhd,khd->hqk/dot_general | solution.py:136
  619.8 8.2 %fusion.18 = bf16[128,1,4,64]{0,3,2,1:T(8,128)(2,1)} fusion(f32[4,8192,128]{2,1,0:T(8,128)} %exponential_select_fusion, bf16[8192,2,4,64]{0,3,2,1:T(8,128)(2,1)S(1)} %bitcast.131), kind=kOutput, calls=%fused_computation.110 | convolution fusion | flops 541097984 | bytes 21037056 | tf_op jit(solution)/shard_map/hqk,qhd->khd/dot_general | solution.py:143
  628.1 12.7 %fusion.22 = bf16[128,1,4,64]{0,3,2,1:T(8,128)(2,1)} fusion(f32[4,8192,128]{2,1,0:T(8,128)} %exponential_select_fusion, f32[4,8192]{1,0:T(4,128)} %bitcast.152, bf16[8192,2,4,64]{0,3,2,1:T(8,128)(2,1)} %bitcast.128, bf16[128,2,4,64]{0,3,2,1:T(8,128)(2,1)} %bitcast.145), kind=kOutput, calls=%fused_computation.112 | convolution fusion | flops 1090551808 | bytes 25427968 | tf_op jit(solution)/shard_map/hqk,qhd->khd/dot_general | solution.py:142
  642.9 89.6 %all-reduce.4.cloned.1.call-done = bf16[128,1536]{1,0:T(8,128)(2,1)} async-done(((bf16[128,1536]{1,0:T(8,128)(2,1)}), bf16[128,1536]{1,0:T(8,128)(2,1)}) %all-reduce.4.cloned.1.call-update) | async-done | bytes 393232 | tf_op jit(solution)/shard_map/psum | solution.py:229
  734.9 3.2 collective-permute-start.2
  739.5 3.7 collective-permute-done.3
  743.3 1.9 fusion.213
  (123 shorter events, 37.8 us)
Async XLA Ops:
  7.2 208.4 %copy-start = (bf16[256,1536]{1,0:T(8,128)(2,1)S(1)}, bf16[256,1536]{1,0:T(8,128)(2,1)}, u32[]{:S(2)}) copy-start(bf16[256,1536]{1,0:T(8,128)(2,1)} %param.19) | copy-start | bytes 2359300
  7.2 192.1 %all-gather.4.cloned.1.call-start = ((), (), s32[]{:S(2)}) async-start(), calls=%async_computation.1 | async-start | bytes 8519680 | tf_op jit(solution)/shard_map/all_gather | solution.py:81
  10.1 14.1 %collective-permute-start = (bf16[3,32,384]{2,1,0:T(8,128)(2,1)}, bf16[3,32,384]{2,1,0:T(8,128)(2,1)S(1)}, u32[]{:S(2)}, u32[]{:S(2)}) collective-permute-start(bf16[3,32,384]{2,1,0:T(8,128)(2,1)} %bitcast), channel_id=1, source_target_pairs={{0,4},{4,8},{8,12},{12,16},{16,20},{20,24},{24,28},{28,32},{32,36}... | collective-permute-start | bytes 221192 | tf_op jit(solution)/shard_map/ppermute | solution.py:27
  14.5 9.7 %collective-permute-start.1 = (bf16[3,32,384]{2,1,0:T(8,128)(2,1)S(1)}, bf16[3,32,384]{2,1,0:T(8,128)(2,1)S(1)}, u32[]{:S(2)}, u32[]{:S(2)}) collective-permute-start(bf16[3,32,384]{2,1,0:T(8,128)(2,1)S(1)} %bitcast.154), channel_id=1, source_target_pairs={{4,0},{8,4},{12,8},{16,12},{20,16},{24,20},{28,24},{32,28},{36,32}... | collective-permute-start | bytes 221192 | tf_op jit(solution)/shard_map/ppermute | solution.py:29
  24.1 11.5 %copy-start.15 = (f32[384]{0:T(512)}, f32[384]{0:T(512)S(1)}, u32[]{:S(2)}) copy-start(f32[384]{0:T(512)S(1)} %get-tuple-element.73) | copy-start | bytes 4612
  24.1 11.5 %copy-start.16 = (f32[384]{0:T(512)}, f32[384]{0:T(512)S(1)}, u32[]{:S(2)}) copy-start(f32[384]{0:T(512)S(1)} %get-tuple-element.74) | copy-start | bytes 4612
  24.1 11.5 %copy-start.17 = (f32[384]{0:T(512)}, f32[384]{0:T(512)S(1)}, u32[]{:S(2)}) copy-start(f32[384]{0:T(512)S(1)} %get-tuple-element.75) | copy-start | bytes 4612
  24.2 11.5 %copy-start.18 = (f32[384]{0:T(512)}, f32[384]{0:T(512)S(1)}, u32[]{:S(2)}) copy-start(f32[384]{0:T(512)S(1)} %get-tuple-element.76) | copy-start | bytes 4612
  24.2 11.5 %copy-start.19 = (f32[384]{0:T(512)}, f32[384]{0:T(512)S(1)}, u32[]{:S(2)}) copy-start(f32[384]{0:T(512)S(1)} %get-tuple-element.91) | copy-start | bytes 4612
  24.2 11.5 %copy-start.20 = (f32[384]{0:T(512)}, f32[384]{0:T(512)S(1)}, u32[]{:S(2)}) copy-start(f32[384]{0:T(512)S(1)} %get-tuple-element.92) | copy-start | bytes 4612
  24.2 11.5 %copy-start.21 = (f32[384]{0:T(512)}, f32[384]{0:T(512)S(1)}, u32[]{:S(2)}) copy-start(f32[384]{0:T(512)S(1)} %get-tuple-element.93) | copy-start | bytes 4612
  24.2 11.5 %copy-start.22 = (f32[384]{0:T(512)}, f32[384]{0:T(512)S(1)}, u32[]{:S(2)}) copy-start(f32[384]{0:T(512)S(1)} %get-tuple-element.94) | copy-start | bytes 4612
  24.2 11.5 %copy-start.23 = (f32[384]{0:T(512)}, f32[384]{0:T(512)S(1)}, u32[]{:S(2)}) copy-start(f32[384]{0:T(512)S(1)} %get-tuple-element.95) | copy-start | bytes 4612
  35.4 162.4 %copy-start.26 = (f32[128]{0:T(128)}, f32[128]{0:T(128)S(1)}, u32[]{:S(2)}) copy-start(f32[128]{0:T(128)S(1)} %broadcast_multiply_fusion.3) | copy-start | bytes 1540
  35.7 162.1 %copy-start.27 = (f32[128]{0:T(128)}, f32[128]{0:T(128)S(1)}, u32[]{:S(2)}) copy-start(f32[128]{0:T(128)S(1)} %add_rsqrt_fusion) | copy-start | bytes 1540
  41.4 217.0 %reduce-scatter.4.cloned.1.call-start = ((), (), s32[]{:S(2)}) async-start(), calls=%async_computation.4 | async-start | bytes 491520
  218.6 379.2 %all-gather.6.cloned.1.call-start = ((), (), s32[]{:S(2)}) async-start(), calls=%async_computation.2 | async-start | bytes 8519680 | tf_op jit(solution)/shard_map/all_gather | solution.py:218
  271.6 461.0 %all-reduce.4.cloned.1.call-start = ((), (), s32[]{:S(2)}) async-start(), calls=%async_computation.3 | async-start | bytes 786432 | tf_op jit(solution)/shard_map/psum | solution.py:229
  628.1 118.5 %copy-start.1 = (bf16[256,1536]{1,0:T(8,128)(2,1)S(1)}, bf16[256,1536]{1,0:T(8,128)(2,1)}, u32[]{:S(2)}) copy-start(bf16[256,1536]{1,0:T(8,128)(2,1)} %param.19) | copy-start | bytes 2359300
  628.1 115.2 %copy-start.7 = (f32[384]{0:T(512)S(1)}, f32[384]{0:T(512)}, u32[]{:S(2)}) copy-start(f32[384]{0:T(512)} %get-tuple-element.29) | copy-start | bytes 4612
  628.1 115.2 %copy-start.8 = (f32[384]{0:T(512)S(1)}, f32[384]{0:T(512)}, u32[]{:S(2)}) copy-start(f32[384]{0:T(512)} %get-tuple-element.30) | copy-start | bytes 4612
  628.1 115.2 %copy-start.9 = (f32[384]{0:T(512)S(1)}, f32[384]{0:T(512)}, u32[]{:S(2)}) copy-start(f32[384]{0:T(512)} %get-tuple-element.31) | copy-start | bytes 4612
  734.9 4.6 collective-permute-start.2
  738.1 5.1 collective-permute-start.3
  (14 other events, 114.4 us)
Sparse Core Ops, SparseCore 0:
  41.5 134.2 all-gather.3
  218.8 39.5 reduce-scatter.3
  271.7 145.6 all-gather.5
  643.1 89.4 all-reduce.3
where the time goes:
time: 757 us; the launch traced here: 753 us
  blocking collectives  479 us (63%)
  waiting for transfers between devices  128 us (17%)
  matrix products  60.8 us (8%)
  local copies, waits for them, and re-layouts  33.8 us (4%)
  other arithmetic  26.1 us (3%)
  between operations  15 us (2%)
  starting transfers between devices  10.3 us (1%)
    all_gather x1, blocking collectives, over_keys(): lax.all_gather(tissue, 'ctx', axis=0, tiled=True)  156 us
    all_gather x1, blocking collectives, on_device(): lax.all_gather(log_total.T, 'ctx', axis=0, tiled=True)  155 us
    all_gather x1, blocking collectives, on_device(): lax.all_gather(shift.T, 'ctx', axis=0, tiled=True)  153 us
    psum x1, waiting for transfers between devices, on_device(): lax.psum(input_part.astype(jnp.bfloat16), 'head').astype(jnp.float32)  89.6 us
    unnamed x5, waiting for transfers between devices  34.9 us
  transfers between devices with their start and end apart: 8, of which 4 were waited for; matrix products, arithmetic and copies ran while one was open for 4% of the time, Pallas kernels for 0%

commit v1 on v0

v1 whole, which is shorter than its diff:
```python
import jax
import jax.numpy as jnp
from jax import lax
from jax.experimental import pallas as pl
from jax.experimental.pallas import tpu as pltpu
from jax.sharding import PartitionSpec as P

HEAD_DIM = 64
GRID_COLS = 32
ROWS = 128
QUADS = 4
BLOCKS = 16
SPAN = BLOCKS * ROWS
CHUNK = 256
HALF = ROWS // 2
WHOLE = 60 << 20

DROP_LEVEL = 103
KEEP_SCALE = 1024.0 / 921.0
NEG = -1e30
EPS = 1e-05
DEAD = 2.0**100

MESH = pl.DeviceIdType.MESH
ANY = pl.BlockSpec(memory_space=pl.ANY)
NT = (((1,), (1,)), ((), ()))


def struct(shape, dtype=jnp.bfloat16):
    return jax.ShapeDtypeStruct(shape, dtype)


def place():
    ctx = lax.axis_index("ctx")
    return ctx, ctx // 16, (ctx // 8) % 2, ctx % 8


def query_peers():
    ctx, x, y, z = place()
    mine = ctx % 16
    peers = []
    for step in range(1, 16):
        to = (mine + step) % 16
        peers.append((x * 16 + to, to, 2 * (to // 8) + to % 2))
    return mine, 2 * y + z % 2, peers


def key_peers():
    ctx, x, y, z = place()
    mine = x * 4 + y * 2 + z % 2
    peers = []
    for step in range(1, 16):
        to = (mine + step) % 16
        peers.append((((to // 4) * 2 + (to // 2) % 2) * 8 + (z // 2) * 2 + to % 2, to, to % 4))
    return mine, 2 * y + z % 2, peers


def stat_peers():
    ctx, x, y, z = place()
    mine = z // 2
    peers = []
    for step in range(1, 4):
        to = (mine + step) % 4
        peers.append(((ctx // 8) * 8 + to * 2 + z % 2, to))
    return mine, peers


def head_peers():
    mine = lax.axis_index("head")
    return mine, [(mine + step) % 4 for step in range(1, 4)]


class Copies:
    def __init__(self, send, recv, own):
        self.send, self.recv, self.own = send, recv, own
        self.far, self.near = [], []

    def to(self, src, dst, device):
        at = len(self.far)
        copy = pltpu.make_async_remote_copy(
            src_ref=src,
            dst_ref=dst,
            send_sem=self.send.at[at],
            recv_sem=self.recv.at[at],
            device_id=device,
            device_id_type=MESH,
        )
        copy.start()
        self.far.append(copy)
        return copy

    def here(self, src, dst):
        copy = pltpu.make_async_copy(src, dst, self.own.at[len(self.near)])
        copy.start()
        self.near.append(copy)
        return copy

    def sent(self):
        for copy in self.far:
            copy.wait_send()


def received(copies):
    for copy in copies:
        copy.wait_recv()


def ring_ids():
    ctx = lax.axis_index("ctx")
    return (ctx + 63) % 64, (ctx + 1) % 64


def everyone():
    before, after = ring_ids()
    ids = [{"ctx": before}, {"ctx": after}]
    ids += [{"head": h} for h in head_peers()[1]]
    ids += [{"ctx": c} for c, _, _ in query_peers()[2]]
    return ids + [{"ctx": c} for c, _, _ in key_peers()[2]]


def announce(ids):
    barrier = pltpu.get_barrier_semaphore()
    for device in ids:
        pl.semaphore_signal(barrier, inc=1, device_id=device, device_id_type=MESH)


def all_here(ids):
    pl.semaphore_wait(pltpu.get_barrier_semaphore(), len(ids))


def stat_kernel(stats, stats_all, send, recv, own):
    mine, peers = stat_peers()
    ids = [{"ctx": c} for c, _ in peers]
    announce(ids)
    copies = Copies(send, recv, own)
    kept = copies.here(stats.at[pl.ds(0, 32)], stats_all.at[mine])
    all_here(ids)
    for device in ids:
        copies.to(stats.at[pl.ds(0, 32)], stats_all.at[mine], device)
    kept.wait()
    received(copies.far)
    copies.sent()


def lanes(rows, width=128):
    return lax.broadcasted_iota(jnp.int32, (rows, width), 1)


def normalised(full_ref):
    parts = [full_ref[i].astype(jnp.float32) for i in range(QUADS)]
    width = QUADS * parts[0].shape[1]
    mean = sum(jnp.sum(p, axis=1, keepdims=True) for p in parts) / width
    parts = [p - mean for p in parts]
    var = sum(jnp.sum(p * p, axis=1, keepdims=True) for p in parts) / width
    spread = lax.rsqrt(var + EPS)
    return [p * spread for p in parts], spread


def fold(top, bottom, low_half):
    low = lanes(top.shape[0]) < HEAD_DIM
    if low_half:
        return jnp.where(low, top, pltpu.roll(bottom, 64, 1))
    return jnp.where(low, pltpu.roll(top, 64, 1), bottom)


def fold_rows(block, low_half):
    return fold(block[0:64], block[64:128], low_half)


def unfold_rows(packed, low_half):
    moved = pltpu.roll(packed, 64, 1)
    return jnp.concatenate([packed, moved] if low_half else [moved, packed], axis=0)


def query_block(q_ref, d_ref, at):
    q = unfold_rows(q_ref[at].astype(jnp.float32), False)
    d = unfold_rows(d_ref[at].astype(jnp.float32), True)
    return jnp.where(lanes(ROWS) < HEAD_DIM, d, q)


def build_keys(vk_ref, keys):
    for block in range(BLOCKS):
        rows = slice(block * ROWS, (block + 1) * ROWS)
        part = vk_ref[block].astype(jnp.float32)
        dead = part[:, 0:1] > DEAD / 2
        lane = lanes(ROWS)
        bias = jnp.where(dead, NEG, 0.0)
        aux = jnp.where(lane == 0, bias, jnp.where(lane < 4, 1.0, 0.0))
        keys[rows, 0:128] = jnp.where(dead, 0.0, part).astype(jnp.bfloat16)
        keys[rows, 128:256] = aux.astype(jnp.bfloat16)


def query_chunk(q_ref, d_ref):
    return jnp.concatenate([query_block(q_ref, d_ref, i) for i in range(CHUNK // ROWS)], axis=0)


def forward_kernel(q_ref, d_ref, vk_ref, p_ref, o_ref, stat_ref, keys):
    step = pl.program_id(0)

    @pl.when(step == 0)
    def _():
        build_keys(vk_ref, keys)

    q = query_chunk(q_ref, d_ref)
    lane = lanes(CHUNK)
    left = jnp.concatenate(
        [jnp.where(lane >= HEAD_DIM, q * 0.125, 0.0), jnp.where(lane == 0, 1.0, 0.0)], axis=1
    ).astype(jnp.bfloat16)
    scores = lax.dot_general(left, keys[...], NT, preferred_element_type=jnp.float32)
    highest = jnp.max(scores, axis=1, keepdims=True)
    weights = jnp.exp(scores - highest).astype(jnp.bfloat16)
    p_ref[...] = weights
    summed = jnp.dot(weights, keys[...], preferred_element_type=jnp.float32)
    totals = summed[:, 129:130]
    attended = summed[:, 0:128] / totals
    o_ref[...] = attended
    inner = jnp.sum(jnp.where(lane < HEAD_DIM, attended * q, 0.0), axis=1, keepdims=True)
    log_total = highest + jnp.log(totals)
    table = jnp.where(
        lane == 0, log_total, jnp.where(lane == 1, inner, jnp.where(lane == 2, highest, 0.0))
    ).T
    for kind in range(3):
        for half in range(2):
            stat_ref[pl.ds(16 * kind + 2 * step + half, 1), :] = table[
                kind : kind + 1, half * 128 : half * 128 + 128
            ]


def backward_kernel(
    q_ref,
    d_ref,
    vk_ref,
    p_ref,
    o_ref,
    stat_ref,
    stats_ref,
    out_ref,
    query_ref,
    grad_ref,
    keys,
    table,
    value_acc,
    key_acc,
):
    step = pl.program_id(0)

    @pl.when(step == 0)
    def _():
        build_keys(vk_ref, keys)
        value_acc[...] = jnp.zeros_like(value_acc)
        key_acc[...] = jnp.zeros_like(key_acc)
        logs = [stats_ref[i, 0:16, :] for i in range(4)]
        top = jnp.maximum(jnp.maximum(logs[0], logs[1]), jnp.maximum(logs[2], logs[3]))
        total = top + jnp.log(sum(jnp.exp(part - top) for part in logs))
        shift = sum(jnp.exp(logs[i] - total) * stats_ref[i, 16:32, :] for i in range(4))
        share = jnp.exp(stat_ref[0:16, :] - total)
        factor = jnp.exp(stat_ref[32:48, :] - total)
        rows = jnp.concatenate([share, shift, factor, jnp.zeros((80, 128), jnp.float32)], axis=0)
        table[...] = rows.T

    lane = lanes(ROWS)

    def column(kind):
        return jnp.concatenate(
            [
                jnp.sum(
                    jnp.where(lane == 16 * kind + 2 * step + half, table[...], 0.0),
                    axis=1,
                    keepdims=True,
                )
                for half in range(2)
            ],
            axis=0,
        )

    share, shift, factor = column(0), column(1), column(2)
    lane = lanes(CHUNK)
    qd = query_chunk(q_ref, d_ref)
    high = shift.astype(jnp.bfloat16).astype(jnp.float32)
    middle = (shift - high).astype(jnp.bfloat16).astype(jnp.float32)
    low = shift - high - middle
    extra = jnp.where(
        lane == 1, -high, jnp.where(lane == 2, -middle, jnp.where(lane == 3, -low, 0.0))
    )
    left = jnp.concatenate([jnp.where(lane < HEAD_DIM, qd, 0.0), extra], axis=1).astype(
        jnp.bfloat16
    )
    dprob = lax.dot_general(left, keys[...], NT, preferred_element_type=jnp.float32)
    weights = p_ref[...]
    slope = (weights.astype(jnp.float32) * dprob).astype(jnp.bfloat16)
    query_grad = jnp.dot(slope, keys[:, 0:128], preferred_element_type=jnp.float32)
    query_grad = query_grad * (factor * 0.125)
    attended = o_ref[...] * share
    for block in range(CHUNK // ROWS):
        rows = slice(block * ROWS, (block + 1) * ROWS)
        query_ref[block] = fold_rows(query_grad[rows], False).astype(jnp.bfloat16)
        out_ref[block] = fold_rows(attended[rows], True).astype(jnp.bfloat16)
    scaled = (qd * factor * jnp.where(lane < HEAD_DIM, 1.0, 0.125)).T.astype(jnp.bfloat16)
    value_acc[...] += jnp.dot(scaled[0:64], weights, preferred_element_type=jnp.float32)
    key_acc[...] += jnp.dot(scaled[64:128], slope, preferred_element_type=jnp.float32)

    @pl.when(step == pl.num_programs(0) - 1)
    def _():
        for block in range(BLOCKS):
            cols = slice(block * ROWS, (block + 1) * ROWS)
            both = jnp.concatenate([value_acc[:, cols], key_acc[:, cols]], axis=0)
            grad_ref[block] = both.T.astype(jnp.bfloat16)


def attention_forward(query_all, grad_all, key_all):
    per = CHUNK // ROWS
    return pl.pallas_call(
        forward_kernel,
        grid=(SPAN // CHUNK,),
        in_specs=[
            pl.BlockSpec((per, HALF, 128), lambda i: (i, 0, 0)),
            pl.BlockSpec((per, HALF, 128), lambda i: (i, 0, 0)),
            pl.BlockSpec((BLOCKS, ROWS, 128), lambda i: (0, 0, 0)),
        ],
        out_specs=[
            pl.BlockSpec((CHUNK, SPAN), lambda i: (i, 0)),
            pl.BlockSpec((CHUNK, 128), lambda i: (i, 0)),
            pl.BlockSpec((48, 128), lambda i: (0, 0)),
        ],
        out_shape=[
            struct((SPAN, SPAN)),
            struct((SPAN, 128), jnp.float32),
            struct((48, 128), jnp.float32),
        ],
        scratch_shapes=[pltpu.VMEM((SPAN, 256), jnp.bfloat16)],
        compiler_params=pltpu.CompilerParams(vmem_limit_bytes=WHOLE),
    )(query_all, grad_all, key_all)


def attention_backward(query_all, grad_all, key_all, weights, attended, stat, stats):
    per = CHUNK // ROWS
    return pl.pallas_call(
        backward_kernel,
        grid=(SPAN // CHUNK,),
        in_specs=[
            pl.BlockSpec((per, HALF, 128), lambda i: (i, 0, 0)),
            pl.BlockSpec((per, HALF, 128), lambda i: (i, 0, 0)),
            pl.BlockSpec((BLOCKS, ROWS, 128), lambda i: (0, 0, 0)),
            pl.BlockSpec((CHUNK, SPAN), lambda i: (i, 0)),
            pl.BlockSpec((CHUNK, 128), lambda i: (i, 0)),
            pl.BlockSpec((48, 128), lambda i: (0, 0)),
            pl.BlockSpec((4, 32, 128), lambda i: (0, 0, 0)),
        ],
        out_specs=[
            pl.BlockSpec((per, HALF, 128), lambda i: (i, 0, 0)),
            pl.BlockSpec((per, HALF, 128), lambda i: (i, 0, 0)),
            pl.BlockSpec((BLOCKS, ROWS, 128), lambda i: (0, 0, 0)),
        ],
        out_shape=[
            struct((BLOCKS, HALF, 128)),
            struct((BLOCKS, HALF, 128)),
            struct((BLOCKS, ROWS, 128)),
        ],
        scratch_shapes=[
            pltpu.VMEM((SPAN, 256), jnp.bfloat16),
            pltpu.VMEM((128, 128), jnp.float32),
            pltpu.VMEM((HEAD_DIM, SPAN), jnp.float32),
            pltpu.VMEM((HEAD_DIM, SPAN), jnp.float32),
        ],
        compiler_params=pltpu.CompilerParams(vmem_limit_bytes=WHOLE),
    )(query_all, grad_all, key_all, weights, attended, stat, stats)


def keep_mask(anchor, counter, row_ids, col_ids):
    mixed = (
        row_ids * jnp.int32(374761393)
        + col_ids * jnp.int32(668265263)
        + anchor * jnp.int32(1274126177)
        + counter
    )
    mixed = jnp.bitwise_xor(mixed, lax.shift_right_logical(mixed, jnp.full_like(mixed, 15)))
    mixed = mixed * jnp.int32(16777619)
    mixed = jnp.bitwise_xor(mixed, lax.shift_right_logical(mixed, jnp.full_like(mixed, 13)))
    mixed = mixed * jnp.int32(1274126177)
    mixed = jnp.bitwise_xor(mixed, lax.shift_right_logical(mixed, jnp.full_like(mixed, 16)))
    return (jnp.bitwise_and(mixed, jnp.int32(1023)) >= DROP_LEVEL).astype(jnp.float32)


def own_keep(seed_ref, rows, width):
    row_ids = lax.axis_index("ctx") * rows + lax.broadcasted_iota(jnp.int32, (rows, width), 0)
    col_ids = lax.axis_index("head") * width + lax.broadcasted_iota(jnp.int32, (rows, width), 1)
    return keep_mask(seed_ref[0], seed_ref[1], row_ids, col_ids)


def alive_column(tissue_ref):
    row = tissue_ref[...].astype(jnp.float32)
    return jnp.broadcast_to(row, (ROWS, ROWS)).T


def merged_tap(taps_ref, row, col, cols):
    tap = taps_ref[row * 7 + col : row * 7 + col + 1, cols]
    if 1 <= row <= 5 and 1 <= col <= 5:
        at = 49 + (row - 1) * 5 + col - 1
        tap = tap + taps_ref[at : at + 1, cols]
    if 2 <= row <= 4 and 2 <= col <= 4:
        at = 74 + (row - 2) * 3 + col - 2
        tap = tap + taps_ref[at : at + 1, cols]
    return tap


def depthwise(flipped, field, above, below, taps_ref, bias, alive, padded):
    ctx = lax.axis_index("ctx")
    width = field.shape[1]
    grid_rows = ROWS // GRID_COLS
    has_above = jnp.where(ctx > 0, 1.0, 0.0)
    has_below = jnp.where(ctx < 63, 1.0, 0.0)
    field = field.astype(jnp.float32)
    padded[:, 0:8, :] = jnp.zeros((grid_rows + 6, 8, width), jnp.float32)
    padded[:, 40:48, :] = jnp.zeros((grid_rows + 6, 8, width), jnp.float32)
    padded[0:3, 8:40, :] = (above.astype(jnp.float32) * has_above).reshape(3, GRID_COLS, width)
    padded[3:7, 8:40, :] = field.reshape(grid_rows, GRID_COLS, width)
    padded[7:10, 8:40, :] = (below.astype(jnp.float32) * has_below).reshape(3, GRID_COLS, width)
    for start in range(0, width, 128):
        cols = slice(start, start + 128)
        total = field[:, cols].reshape(grid_rows, GRID_COLS, 128)
        if bias is not None:
            total = total + bias[:, cols].reshape(1, 1, 128)
        for col in range(7):
            moved = padded[:, 5 + col : 37 + col, cols]
            for row in range(7):
                if flipped:
                    tap = merged_tap(taps_ref, 6 - row, 6 - col, cols)
                else:
                    tap = merged_tap(taps_ref, row, col, cols)
                total = total + tap.reshape(1, 1, 128) * moved[row : row + grid_rows]
        yield cols, total.reshape(ROWS, 128) * alive


def front_kernel(
    seed_ref,
    tokens_in,
    tissue_in,
    grad_in,
    taps_in,
    bias_in,
    gain_in,
    w_in,
    w_out_in,
    query_all,
    grad_all,
    key_all,
    full_all,
    tokens,
    tissue,
    grad,
    taps,
    bias,
    gain,
    w,
    w_out,
    masked,
    above,
    below,
    drop_full,
    full,
    query_part,
    grad_part,
    key_part,
    padded,
    send,
    recv,
    own,
):
    rows, width = tokens.shape
    ids = everyone()
    announce(ids)
    copies = Copies(send, recv, own)
    first = [
        copies.here(src, dst)
        for src, dst in ((tokens_in, tokens), (tissue_in, tissue), (grad_in, grad))
    ]
    for_conv = [copies.here(taps_in, taps), copies.here(bias_in, bias)]
    for_grad = [copies.here(w_out_in, w_out)]
    for_project = [copies.here(gain_in, gain), copies.here(w_in, w)]
    before, after = ring_ids()
    mine, heads = head_peers()
    keep = own_keep(seed_ref, rows, width)
    for copy in first:
        copy.wait()
    alive = alive_column(tissue)
    column = alive[:, 0:1]
    masked[...] = (tokens[...].astype(jnp.float32) * column).astype(jnp.bfloat16)
    all_here(ids)
    halos = [
        copies.to(masked.at[pl.ds(32, 96)], above, {"ctx": after}),
        copies.to(masked.at[pl.ds(0, 96)], below, {"ctx": before}),
    ]
    upstream = grad[...].astype(jnp.float32) * column
    drop_full[mine] = (upstream * keep * KEEP_SCALE).astype(jnp.bfloat16)
    drops = [copies.to(drop_full.at[mine], drop_full.at[mine], {"head": h}) for h in heads]

    for copy in for_conv:
        copy.wait()
    received(halos)
    for cols, part in depthwise(
        False, masked[...], above[...], below[...], taps, bias[...], alive, padded
    ):
        full[mine, :, cols] = part.astype(jnp.bfloat16)
    parts = [copies.to(full.at[mine], full.at[mine], {"head": h}) for h in heads]

    q_mine, slot, q_peers = query_peers()
    k_mine, _, k_peers = key_peers()
    for copy in for_grad:
        copy.wait()
    received(drops)
    out_grad = sum(
        lax.dot_general(
            drop_full[i],
            w_out[:, i * width : (i + 1) * width],
            NT,
            preferred_element_type=jnp.float32,
        )
        for i in range(QUADS)
    )
    for j in range(QUADS):
        pair = out_grad[:, 128 * (j // 2) : 128 * (j // 2) + 128]
        grad_part[j] = fold_rows(pair, j % 2 == 0).astype(jnp.bfloat16)
    landing = [
        copies.to(grad_part.at[h], grad_all.at[q_mine], {"ctx": c}) for c, _, h in q_peers
    ]
    local = [copies.here(grad_part.at[slot], grad_all.at[q_mine])]

    for copy in for_project:
        copy.wait()
    received(parts)
    local.append(copies.here(full, full_all))
    unit, _ = normalised(full)
    sums = [jnp.zeros((rows, w.shape[2]), jnp.float32) for _ in range(3)]
    for i in range(QUADS):
        span = slice(i * width, (i + 1) * width)
        normed = (unit[i] * gain[:, span]).astype(jnp.bfloat16)
        for k in range(3):
            sums[k] = sums[k] + jnp.dot(normed, w[k, span, :], preferred_element_type=jnp.float32)
    low = lanes(ROWS) < HEAD_DIM
    dead = alive == 0.0
    for j in range(QUADS):
        q, k, v = (part[:, 128 * (j // 2) : 128 * (j // 2) + 128] for part in sums)
        query_part[j] = fold_rows(q, j % 2 == 0).astype(jnp.bfloat16)
        if j % 2 == 0:
            both = jnp.where(low, v, pltpu.roll(k, 64, 1))
        else:
            both = jnp.where(low, pltpu.roll(v, 64, 1), k)
        key_part[j] = jnp.where(dead, DEAD, both).astype(jnp.bfloat16)
    for (qc, _, qh), (kc, _, kh) in zip(q_peers, k_peers):
        landing.append(copies.to(key_part.at[kh], key_all.at[k_mine], {"ctx": kc}))
        landing.append(copies.to(query_part.at[qh], query_all.at[q_mine], {"ctx": qc}))
    local.append(copies.here(query_part.at[slot], query_all.at[q_mine]))
    local.append(copies.here(key_part.at[slot], key_all.at[k_mine]))
    for copy in local:
        copy.wait()
    received(landing)
    copies.sent()


def back_kernel(
    seed_ref,
    attended_in,
    query_in,
    key_in,
    full_in,
    tissue_in,
    grad_in,
    taps_in,
    gain_in,
    w_in,
    w_out_in,
    encoded_out,
    tokens_out,
    tissue,
    grad,
    taps,
    gain,
    w,
    w_out,
    full,
    attended_all,
    query_all,
    key_all,
    grad_send,
    grad_recv,
    branch_send,
    branch_recv,
    sums_send,
    sums_recv,
    source,
    above,
    below,
    encoded,
    result,
    padded,
    send,
    recv,
    own,
):
    rows, width = grad.shape
    ids = everyone()
    announce(ids)
    copies = Copies(send, recv, own)
    q_mine, _, q_peers = query_peers()
    k_mine, _, k_peers = key_peers()
    first = [
        copies.here(src, dst)
        for src, dst in ((tissue_in, tissue), (grad_in, grad), (full_in, full), (gain_in, gain))
    ]
    later = [copies.here(src, dst) for src, dst in ((w_in, w), (w_out_in, w_out), (taps_in, taps))]
    kept = [
        copies.here(query_in.at[q_mine], query_all.at[q_mine]),
        copies.here(key_in.at[k_mine], key_all.at[k_mine]),
        copies.here(attended_in.at[q_mine], attended_all.at[q_mine]),
    ]
    all_here(ids)
    grads_back, outs_back = [], []
    for (qc, qd, _), (kc, kd, _) in zip(q_peers, k_peers):
        grads_back.append(copies.to(key_in.at[kd], key_all.at[k_mine], {"ctx": kc}))
        grads_back.append(copies.to(query_in.at[qd], query_all.at[q_mine], {"ctx": qc}))
    for qc, qd, _ in q_peers:
        outs_back.append(copies.to(attended_in.at[qd], attended_all.at[q_mine], {"ctx": qc}))

    mine, heads = head_peers()
    before, after = ring_ids()
    for copy in first + later:
        copy.wait()
    keep = own_keep(seed_ref, rows, width)
    alive = alive_column(tissue)
    column = alive[:, 0:1]
    unit, spread = normalised(full)
    low = lanes(ROWS) < HEAD_DIM

    def total(ref, slots):
        parts = [ref[s].astype(jnp.float32) for s in slots]
        return (parts[0] + parts[1]) + (parts[2] + parts[3])

    def queries(ref):
        heads_ = []
        for j in range(QUADS):
            packed = total(ref, [8 * (j // 2) + 2 * k + j % 2 for k in range(4)])
            heads_.append(unfold_rows(packed, j % 2 == 0))
        pairs = [jnp.where(low, heads_[2 * p], heads_[2 * p + 1]) for p in range(2)]
        return jnp.concatenate(pairs, axis=1).astype(jnp.bfloat16)

    for copy in kept:
        copy.wait()
    received(grads_back)
    both = [total(key_all, [4 * k + j for k in range(4)]) for j in range(QUADS)]
    values = [jnp.where(low, both[2 * p], pltpu.roll(both[2 * p + 1], 64, 1)) for p in range(2)]
    keys = [jnp.where(low, pltpu.roll(both[2 * p], 64, 1), both[2 * p + 1]) for p in range(2)]
    grads = [
        queries(query_all),
        jnp.concatenate(keys, axis=1).astype(jnp.bfloat16),
        jnp.concatenate(values, axis=1).astype(jnp.bfloat16),
    ]
    plain = jnp.zeros((ROWS, 1), jnp.float32)
    crossed = jnp.zeros((ROWS, 1), jnp.float32)
    for i in range(QUADS):
        span = slice(i * width, (i + 1) * width)
        part = sum(
            lax.dot_general(grads[k], w[k, span, :], NT, preferred_element_type=jnp.float32)
            for k in range(3)
        )
        grad_send[i] = part.astype(jnp.bfloat16)
        scaled = part * gain[:, span]
        plain = plain + jnp.sum(scaled, axis=1, keepdims=True)
        crossed = crossed + jnp.sum(scaled * unit[i], axis=1, keepdims=True)
    lane = lanes(ROWS)
    sums_send[...] = jnp.where(lane == 0, plain, jnp.where(lane == 1, crossed, 0.0)).T[0:8]
    scattered = []
    for h in heads:
        scattered.append(copies.to(grad_send.at[h], grad_recv.at[mine], {"head": h}))
        scattered.append(copies.to(sums_send, sums_recv.at[mine], {"head": h}))
    grad_recv[mine] = grad_send[mine]
    sums_recv[mine] = sums_send[...]

    received(outs_back)
    attended = queries(attended_all)
    for i in range(QUADS):
        span = slice(i * width, (i + 1) * width)
        branch_send[i] = jnp.dot(
            attended, w_out[:, span], preferred_element_type=jnp.float32
        ).astype(jnp.bfloat16)
    branches = [copies.to(branch_send.at[h], branch_recv.at[mine], {"head": h}) for h in heads]
    branch_recv[mine] = branch_send[mine]

    own_unit = jnp.zeros((ROWS, width), jnp.float32)
    own_gain = jnp.zeros((1, width), jnp.float32)
    for i in range(QUADS):
        own_unit = jnp.where(mine == i, unit[i], own_unit)
        own_gain = jnp.where(mine == i, gain[:, i * width : (i + 1) * width], own_gain)
    received(scattered)
    sums = (sums_recv[0] + sums_recv[1]) + (sums_recv[2] + sums_recv[3])
    means = jnp.concatenate([sums, jnp.zeros((120, 128), jnp.float32)], axis=0).T / (QUADS * width)
    scaled = total(grad_recv, range(QUADS)) * own_gain
    inner = scaled - means[:, 0:1] - own_unit * means[:, 1:2]
    upstream = grad[...].astype(jnp.float32) * column
    source[...] = ((upstream + inner * spread) * column).astype(jnp.bfloat16)
    halos = [
        copies.to(source.at[pl.ds(32, 96)], above, {"ctx": after}),
        copies.to(source.at[pl.ds(0, 96)], below, {"ctx": before}),
    ]

    received(branches)
    branch = total(branch_recv, range(QUADS))
    residual = full[mine].astype(jnp.float32)
    encoded[...] = ((residual + branch * keep * KEEP_SCALE) * column).astype(jnp.bfloat16)
    outs = [copies.here(encoded, encoded_out)]

    received(halos)
    for cols, part in depthwise(
        True, source[...], above[...], below[...], taps, None, alive, padded
    ):
        result[:, cols] = part.astype(jnp.bfloat16)
    outs.append(copies.here(result, tokens_out))
    for copy in outs:
        copy.wait()
    copies.sent()


def remote_call(body, collective_id, outs, scratch, far, near, *args):
    smem = pl.BlockSpec(memory_space=pltpu.SMEM)
    return pl.pallas_call(
        body,
        out_shape=outs,
        in_specs=[smem if a.shape == (2,) else ANY for a in args],
        out_specs=[ANY] * len(outs),
        scratch_shapes=scratch
        + [
            pltpu.SemaphoreType.DMA((far,)),
            pltpu.SemaphoreType.DMA((far,)),
            pltpu.SemaphoreType.DMA((near,)),
        ],
        compiler_params=pltpu.CompilerParams(
            collective_id=collective_id, has_side_effects=True, vmem_limit_bytes=WHOLE
        ),
    )(*args)


def on_device(tokens, tissue, conv_taps, conv_bias, ln_gain, w_qkv, w_out, drop_seed, grad_out):
    rows, width = tokens.shape
    gain_row = ln_gain[None, :]
    bias_row = conv_bias[None, :]
    tissue_row = tissue[None, :]
    weights_in = w_qkv.transpose(1, 0, 2)
    half, whole = (HALF, 128), (ROWS, 128)

    def held(shape, dtype=jnp.bfloat16):
        return pltpu.VMEM(shape, dtype)

    def like(array):
        return pltpu.VMEM(array.shape, array.dtype)

    padded = held((rows // GRID_COLS + 6, 48, width), jnp.float32)
    query_all, grad_all, key_all, full = remote_call(
        front_kernel,
        1,
        [
            struct((BLOCKS,) + half),
            struct((BLOCKS,) + half),
            struct((BLOCKS,) + whole),
            struct((QUADS, rows, width)),
        ],
        [
            like(tokens),
            like(tissue_row),
            like(grad_out),
            like(conv_taps),
            like(bias_row),
            like(gain_row),
            like(weights_in),
            like(w_out),
            held((rows, width)),
            held((96, width)),
            held((96, width)),
            held((QUADS, rows, width)),
            held((QUADS, rows, width)),
            held((QUADS,) + half),
            held((QUADS,) + half),
            held((QUADS,) + whole),
            padded,
        ],
        53,
        12,
        drop_seed,
        tokens,
        tissue_row,
        grad_out,
        conv_taps,
        bias_row,
        gain_row,
        weights_in,
        w_out,
    )
    weights, attended, stat = attention_forward(query_all, grad_all, key_all)
    (stats,) = remote_call(
        stat_kernel, 2, [struct((4, 32, 128), jnp.float32)], [], 3, 1, stat
    )
    out_part, query_part, key_part = attention_backward(
        query_all, grad_all, key_all, weights, attended, stat, stats
    )
    encoded, grad_tokens = remote_call(
        back_kernel,
        3,
        [struct((rows, width))] * 2,
        [
            like(tissue_row),
            like(grad_out),
            like(conv_taps),
            like(gain_row),
            like(weights_in),
            like(w_out),
            held((QUADS, rows, width)),
            held((BLOCKS,) + half),
            held((BLOCKS,) + half),
            held((BLOCKS,) + whole),
            held((QUADS, rows, width)),
            held((QUADS, rows, width)),
            held((QUADS, rows, width)),
            held((QUADS, rows, width)),
            held((8, rows), jnp.float32),
            held((QUADS, 8, rows), jnp.float32),
            held((rows, width)),
            held((96, width)),
            held((96, width)),
            held((rows, width)),
            held((rows, width)),
            padded,
        ],
        56,
        12,
        drop_seed,
        out_part,
        query_part,
        key_part,
        full,
        tissue_row,
        grad_out,
        conv_taps,
        gain_row,
        weights_in,
        w_out,
    )
    return (encoded, grad_tokens)


def solution(mesh):
    placed = (
        P("ctx", "head"),
        P("ctx"),
        P(None, "head"),
        P("head"),
        P(),
        P(None, None, "head"),
        P("head", None),
        P(),
        P("ctx", "head"),
    )
    return jax.shard_map(
        on_device,
        mesh=mesh,
        in_specs=placed,
        out_specs=(P("ctx", "head"), P("ctx", "head")),
        check_vma=False,
    )
```

time: 757 us -> 125 us (0.17)
  blocking collectives: 479 us -> 0 us
  waiting for transfers between devices: 128 us -> 0 us
  Pallas kernels: 0 us -> 118 us
  matrix products: 60.8 us -> 0 us
  local copies, waits for them, and re-layouts: 33.8 us -> 5.63 us
  other arithmetic: 26.1 us -> 0 us
  between operations: 15 us -> 0.66 us
  starting transfers between devices: 10.3 us -> 0 us
    all_gather x5 -> x0, blocking collectives: 479 us -> none  [the longest x1 156 us: over_keys(): lax.all_gather(tissue, 'ctx', axis=0, tiled=True)]
    pallas_call x0 -> x5, Pallas kernels: none -> 118 us  [the longest x3 89.3 us: remote_call(): pl.pallas_call(body, out_shape=outs, in_specs=[smem if a.shape == (2,) el...]
    psum x1 -> x0, waiting for transfers between devices: 89.6 us -> none  [on_device(): lax.psum(input_part.astype(jnp.bfloat16), 'head').astype(jnp.float32)]
    dot_general x10 -> x0, matrix products: 60.8 us -> none  [the longest x1 13.8 us: query_grad_step(): jnp.einsum('hqk,khd->qhd', slope, split[:, 0], preferred_element_type=jnp...]
    unnamed x5 -> x0, waiting for transfers between devices: 34.9 us -> none
    all_gather x1 -> x0, local copies, waits for them, and re-layouts: 11.3 us -> none  [on_device(): lax.all_gather(sender, 'ctx', axis=0, tiled=True)]
    ppermute x4 -> x0, starting transfers between devices: 10.1 us -> none  [the longest x2 7.54 us: padded_2(): lax.ppermute(tail, axis, [(i, (i + 1) % count) for i in range(ends)])]
    slice x11 -> x0, local copies, waits for them, and re-layouts: 9.8 us -> none  [the longest x3 2.3 us: depthwise(): kernel[row_off, col_off]]
  transfers between devices with their start and end apart: 8 -> 0, of which waited for: 4 -> 0; matrix products, arithmetic and copies ran while one was open for 4% -> 0% of each run, Pallas kernels for 0% -> 0%
where the time goes in v1:
time: 125 us; the launch traced here: 124 us
  Pallas kernels  118 us (94%)
  local copies, waits for them, and re-layouts  5.63 us (5%)
    pallas_call x3, Pallas kernels, remote_call(): pl.pallas_call(body, out_shape=outs, in_specs=[smem if a.shape == (2,) el...  89.3 us
    pallas_call x1, Pallas kernels, attention_forward(): pl.pallas_call(forward_kernel, grid=(SPAN // CHUNK,), in_specs=[pl.BlockS...  15.4 us
    pallas_call x1, Pallas kernels, attention_backward(): pl.pallas_call(backward_kernel, grid=(SPAN // CHUNK,), in_specs=[pl.Block...  13.5 us
    unnamed x2, local copies, waits for them, and re-layouts  3.09 us

profile of v1, /device:TPU:1, one launch (start us, length us, event | category | flops | bytes accessed | tf_op | source)
XLA Modules:
  0.0 124.5 jit_solution(4742545392441291743)
XLA Ops:
  0.6 1.2 %broadcast_in_dim.10.bias_in = f32[1,384]{1,0:T(1,128)} reshape(f32[384]{0:T(512)} %param.12) | data formatting | bytes 3072 | tf_op jit(solution)/shard_map/broadcast_in_dim | solution.py:744
  1.9 1.3 %broadcast_in_dim.11.gain_in = f32[1,1536]{1,0:T(1,128)} reshape(f32[1536]{0:T(1024)} %param.13) | data formatting | bytes 12288 | tf_op jit(solution)/shard_map/broadcast_in_dim | solution.py:743
  3.2 39.1 %shard_map.104 = (bf16[16,64,128]{2,1,0:T(8,128)(2,1)}, bf16[16,64,128]{2,1,0:T(8,128)(2,1)}, bf16[16,128,128]{2,1,0:T(8,128)(2,1)}, bf16[4,128,384]{2,1,0:T(8,128)(2,1)}) custom-call(s32[2]{0:T(128)} %seed_ref.3, bf16[128,384]{1,0:T(8,128)(2,1)} %tokens_in.1, s32[1,128]{1,0:T(1,128)} %bitcast.4, bf16[128,384]{1,0:T(8,128)(2,1)} %grad_in.3, ...), custom_call_target="tpu_custom_call" | custom-call | tf_op jit(solution)/shard_map/pallas_call | solution.py:724
  42.3 15.4 %shard_map.105 = (bf16[2048,2048]{1,0:T(8,128)(2,1)}, f32[2048,128]{1,0:T(8,128)}, f32[48,128]{1,0:T(8,128)}) custom-call(bf16[16,64,128]{2,1,0:T(8,128)(2,1)} %get-tuple-element.12.q_ref, bf16[16,64,128]{2,1,0:T(8,128)(2,1)} %get-tuple-element.13.d_ref, bf16[16,128,128]{2,1,0:T(8,128)(2,1)} %get-tuple-element.14.vk_ref), custom_call_target="tpu_custom_call" | custom-call | tf_op jit(solution)/shard_map/pallas_call | solution.py:312
  57.7 10.0 %shard_map.106.stats_ref = f32[4,32,128]{2,1,0:T(8,128)} custom-call(f32[48,128]{1,0:T(8,128)} %get-tuple-element.17.stats.stat_ref), custom_call_target="tpu_custom_call" | custom-call | tf_op jit(solution)/shard_map/pallas_call | solution.py:724
  67.7 13.5 %shard_map.107 = (bf16[16,64,128]{2,1,0:T(8,128)(2,1)}, bf16[16,64,128]{2,1,0:T(8,128)(2,1)}, bf16[16,128,128]{2,1,0:T(8,128)(2,1)}) custom-call(bf16[16,64,128]{2,1,0:T(8,128)(2,1)} %get-tuple-element.12.q_ref, bf16[16,64,128]{2,1,0:T(8,128)(2,1)} %get-tuple-element.13.d_ref, bf16[16,128,128]{2,1,0:T(8,128)(2,1)} %get-tuple-element.14.vk_ref, ...), custom_call_target="tpu_custom_call" | custom-call | tf_op jit(solution)/shard_map/pallas_call | solution.py:337
  81.2 40.2 %shard_map.108 = (bf16[128,384]{1,0:T(8,128)(2,1)}, bf16[128,384]{1,0:T(8,128)(2,1)}) custom-call(s32[2]{0:T(128)} %seed_ref.3, bf16[16,64,128]{2,1,0:T(8,128)(2,1)} %get-tuple-element.18.attended_in, bf16[16,64,128]{2,1,0:T(8,128)(2,1)} %get-tuple-element.19.query_in, bf16[16,128,128]{2,1,0:T(8,128)(2,1)} %get-tuple-element.20.key_in, ...), custom_call_target="tpu_custom_call" | custom-call | tf_op jit(solution)/shard_map/pallas_call | solution.py:724
  121.4 1.5 %copy.13 = bf16[128,384]{1,0:T(8,128)(2,1)} copy(bf16[128,384]{1,0:T(8,128)(2,1)} %get-tuple-element.24) | data formatting | bytes 196608
  122.9 1.5 %copy.14 = bf16[128,384]{1,0:T(8,128)(2,1)} copy(bf16[128,384]{1,0:T(8,128)(2,1)} %get-tuple-element.25) | data formatting | bytes 196608

commit v2 on v1

--- a/solution.py
+++ b/solution.py
@@ -14,6 +14,7 @@
 CHUNK = 256
 HALF = ROWS // 2
 WHOLE = 60 << 20
+WIDTHS = (512, 768, 1024, 1536, 2048)
 
 DROP_LEVEL = 103
 KEEP_SCALE = 1024.0 / 921.0
@@ -30,44 +31,54 @@
     return jax.ShapeDtypeStruct(shape, dtype)
 
 
+def div(a, b):
+    return lax.div(a, jnp.int32(b))
+
+
+def mod(a, b):
+    return lax.rem(a, jnp.int32(b))
+
+
 def place():
     ctx = lax.axis_index("ctx")
-    return ctx, ctx // 16, (ctx // 8) % 2, ctx % 8
+    return ctx, div(ctx, 16), mod(div(ctx, 8), 2), mod(ctx, 8)
 
 
 def query_peers():
     ctx, x, y, z = place()
-    mine = ctx % 16
+    mine = mod(ctx, 16)
     peers = []
     for step in range(1, 16):
-        to = (mine + step) % 16
-        peers.append((x * 16 + to, to, 2 * (to // 8) + to % 2))
-    return mine, 2 * y + z % 2, peers
+        to = mod(mine + step, 16)
+        peers.append((x * 16 + to, to, 2 * div(to, 8) + mod(to, 2)))
+    return mine, 2 * y + mod(z, 2), peers
 
 
 def key_peers():
     ctx, x, y, z = place()
-    mine = x * 4 + y * 2 + z % 2
+    mine = x * 4 + y * 2 + mod(z, 2)
+    base = 2 * div(z, 2)
     peers = []
     for step in range(1, 16):
-        to = (mine + step) % 16
-        peers.append((((to // 4) * 2 + (to // 2) % 2) * 8 + (z // 2) * 2 + to % 2, to, to % 4))
-    return mine, 2 * y + z % 2, peers
+        to = mod(mine + step, 16)
+        peers.append((div(to, 2) * 8 + base + mod(to, 2), to, mod(to, 4)))
+    return mine, 2 * y + mod(z, 2), peers
 
 
 def stat_peers():
     ctx, x, y, z = place()
-    mine = z // 2
+    mine = div(z, 2)
+    base = ctx - z + mod(z, 2)
     peers = []
     for step in range(1, 4):
-        to = (mine + step) % 4
-        peers.append(((ctx // 8) * 8 + to * 2 + z % 2, to))
+        to = mod(mine + step, 4)
+        peers.append((base + to * 2, to))
     return mine, peers
 
 
 def head_peers():
     mine = lax.axis_index("head")
-    return mine, [(mine + step) % 4 for step in range(1, 4)]
+    return mine, [mod(mine + step, 4) for step in range(1, 4)]
 
 
 class Copies:
@@ -107,7 +118,7 @@
 
 def ring_ids():
     ctx = lax.axis_index("ctx")
-    return (ctx + 63) % 64, (ctx + 1) % 64
+    return mod(ctx + 63, 64), mod(ctx + 1, 64)
 
 
 def everyone():
@@ -133,10 +144,10 @@
     ids = [{"ctx": c} for c, _ in peers]
     announce(ids)
     copies = Copies(send, recv, own)
-    kept = copies.here(stats.at[pl.ds(0, 32)], stats_all.at[mine])
+    kept = copies.here(stats, stats_all.at[mine])
     all_here(ids)
     for device in ids:
-        copies.to(stats.at[pl.ds(0, 32)], stats_all.at[mine], device)
+        copies.to(stats, stats_all.at[mine], device)
     kept.wait()
     received(copies.far)
     copies.sent()
@@ -175,195 +186,232 @@
 def query_block(q_ref, d_ref, at):
     q = unfold_rows(q_ref[at].astype(jnp.float32), False)
     d = unfold_rows(d_ref[at].astype(jnp.float32), True)
-    return jnp.where(lanes(ROWS) < HEAD_DIM, d, q)
-
-
-def build_keys(vk_ref, keys):
-    for block in range(BLOCKS):
-        rows = slice(block * ROWS, (block + 1) * ROWS)
-        part = vk_ref[block].astype(jnp.float32)
-        dead = part[:, 0:1] > DEAD / 2
-        lane = lanes(ROWS)
-        bias = jnp.where(dead, NEG, 0.0)
-        aux = jnp.where(lane == 0, bias, jnp.where(lane < 4, 1.0, 0.0))
-        keys[rows, 0:128] = jnp.where(dead, 0.0, part).astype(jnp.bfloat16)
-        keys[rows, 128:256] = aux.astype(jnp.bfloat16)
-
-
-def query_chunk(q_ref, d_ref):
-    return jnp.concatenate([query_block(q_ref, d_ref, i) for i in range(CHUNK // ROWS)], axis=0)
-
-
-def forward_kernel(q_ref, d_ref, vk_ref, p_ref, o_ref, stat_ref, keys):
-    step = pl.program_id(0)
-
-    @pl.when(step == 0)
-    def _():
-        build_keys(vk_ref, keys)
-
-    q = query_chunk(q_ref, d_ref)
+    alive = q[:, HEAD_DIM : HEAD_DIM + 1] < DEAD / 2
+    return jnp.where(alive, jnp.where(lanes(ROWS) < HEAD_DIM, d, q), 0.0), alive
+
+
+def extra_lanes(rows, alive):
+    lane = lanes(rows)
+    return jnp.where(lane == 0, jnp.where(alive, 0.0, NEG), jnp.where(lane < 4, 1.0, 0.0))
+
+
+def key_block(vk_ref, at):
+    part = vk_ref[at].astype(jnp.float32)
+    alive = part[:, 0:1] < DEAD / 2
+    return jnp.concatenate([jnp.where(alive, part, 0.0), extra_lanes(ROWS, alive)], axis=1), alive
+
+
+def count(alive):
+    return (jnp.sum(jnp.where(alive, 1.0, 0.0)).astype(jnp.int32) + 15) // 16 * 16
+
+
+def rows_at(start, count_, multiple):
+    return pl.ds(pl.multiple_of(start, multiple), count_)
+
+
+def by_width(size, run):
+    low = 0
+    for width in WIDTHS:
+
+        @pl.when((size > low) & (size <= width))
+        def _(width=width):
+            run(width)
+
+        low = width
+
+
+def scores_of(qd, keys):
     lane = lanes(CHUNK)
     left = jnp.concatenate(
-        [jnp.where(lane >= HEAD_DIM, q * 0.125, 0.0), jnp.where(lane == 0, 1.0, 0.0)], axis=1
+        [jnp.where(lane >= HEAD_DIM, qd * 0.125, 0.0), jnp.where(lane == 0, 1.0, 0.0)], axis=1
     ).astype(jnp.bfloat16)
-    scores = lax.dot_general(left, keys[...], NT, preferred_element_type=jnp.float32)
-    highest = jnp.max(scores, axis=1, keepdims=True)
-    weights = jnp.exp(scores - highest).astype(jnp.bfloat16)
-    p_ref[...] = weights
-    summed = jnp.dot(weights, keys[...], preferred_element_type=jnp.float32)
-    totals = summed[:, 129:130]
-    attended = summed[:, 0:128] / totals
-    o_ref[...] = attended
-    inner = jnp.sum(jnp.where(lane < HEAD_DIM, attended * q, 0.0), axis=1, keepdims=True)
-    log_total = highest + jnp.log(totals)
-    table = jnp.where(
-        lane == 0, log_total, jnp.where(lane == 1, inner, jnp.where(lane == 2, highest, 0.0))
-    ).T
-    for kind in range(3):
-        for half in range(2):
-            stat_ref[pl.ds(16 * kind + 2 * step + half, 1), :] = table[
-                kind : kind + 1, half * 128 : half * 128 + 128
-            ]
+    return lax.dot_general(left, keys, NT, preferred_element_type=jnp.float32)
+
+
+def forward_kernel(q_ref, d_ref, vk_ref, keys, qd, o_ref, stat_ref, starts):
+    nothing = jnp.concatenate(
+        [jnp.zeros((ROWS, 128), jnp.float32), extra_lanes(ROWS, False)], axis=1
+    ).astype(jnp.bfloat16)
+    for block in range(BLOCKS + 1):
+        keys[block * ROWS : (block + 1) * ROWS, :] = nothing
+    qd[...] = jnp.zeros_like(qd)
+    o_ref[...] = jnp.zeros_like(o_ref)
+    stat_ref[...] = jnp.zeros_like(stat_ref)
+    key_end = jnp.int32(0)
+    query_end = jnp.int32(0)
+    for block in range(BLOCKS):
+        part, alive = key_block(vk_ref, block)
+        starts[block] = key_end
+        keys[rows_at(key_end, ROWS, 16), :] = part.astype(jnp.bfloat16)
+        key_end = key_end + count(alive)
+        part, alive = query_block(q_ref, d_ref, block)
+        starts[BLOCKS + block] = query_end
+        qd[rows_at(query_end, ROWS, 16), :] = part.astype(jnp.bfloat16)
+        query_end = query_end + count(alive)
+    starts[2 * BLOCKS] = key_end
+    starts[2 * BLOCKS + 1] = query_end
+    lane = lanes(CHUNK)
+
+    def run(width):
+        def chunk(step, _):
+            rows = rows_at(step * CHUNK, CHUNK, CHUNK)
+            here = qd[rows, :].astype(jnp.float32)
+            scores = scores_of(here, keys[0:width, :])
+            highest = jnp.max(scores, axis=1, keepdims=True)
+            weights = jnp.exp(scores - highest).astype(jnp.bfloat16)
+            summed = jnp.dot(weights, keys[0:width, :], preferred_element_type=jnp.float32)
+            totals = summed[:, 129:130]
+            attended = summed[:, 0:128] / totals
+            o_ref[rows, :] = attended
+            inner = jnp.sum(
+                jnp.where(lane < HEAD_DIM, attended * here, 0.0), axis=1, keepdims=True
+            )
+            log_total = highest + jnp.log(totals)
+            table = jnp.where(lane == 0, log_total, jnp.where(lane == 1, inner, 0.0)).T
+            for kind in range(2):
+                for half in range(2):
+                    stat_ref[pl.ds(16 * kind + 2 * step + half, 1), :] = table[
+                        kind : kind + 1, half * 128 : half * 128 + 128
+                    ]
+            return 0
+
+        lax.fori_loop(0, (query_end + CHUNK - 1) // CHUNK, chunk, 0)
+
+    by_width(key_end, run)
 
 
 def backward_kernel(
-    q_ref,
-    d_ref,
-    vk_ref,
-    p_ref,
+    starts,
+    keys,
+    qd_ref,
     o_ref,
     stat_ref,
     stats_ref,
     out_ref,
     query_ref,
     grad_ref,
-    keys,
     table,
+    query_acc,
     value_acc,
     key_acc,
+    key_rows,
 ):
-    step = pl.program_id(0)
-
-    @pl.when(step == 0)
-    def _():
-        build_keys(vk_ref, keys)
-        value_acc[...] = jnp.zeros_like(value_acc)
-        key_acc[...] = jnp.zeros_like(key_acc)
-        logs = [stats_ref[i, 0:16, :] for i in range(4)]
-        top = jnp.maximum(jnp.maximum(logs[0], logs[1]), jnp.maximum(logs[2], logs[3]))
-        total = top + jnp.log(sum(jnp.exp(part - top) for part in logs))
-        shift = sum(jnp.exp(logs[i] - total) * stats_ref[i, 16:32, :] for i in range(4))
-        share = jnp.exp(stat_ref[0:16, :] - total)
-        factor = jnp.exp(stat_ref[32:48, :] - total)
-        rows = jnp.concatenate([share, shift, factor, jnp.zeros((80, 128), jnp.float32)], axis=0)
-        table[...] = rows.T
-
-    lane = lanes(ROWS)
-
-    def column(kind):
-        return jnp.concatenate(
-            [
-                jnp.sum(
-                    jnp.where(lane == 16 * kind + 2 * step + half, table[...], 0.0),
-                    axis=1,
-                    keepdims=True,
-                )
-                for half in range(2)
-            ],
-            axis=0,
-        )
-
-    share, shift, factor = column(0), column(1), column(2)
+    logs = [stats_ref[i, 0:16, :] for i in range(4)]
+    top = jnp.maximum(jnp.maximum(logs[0], logs[1]), jnp.maximum(logs[2], logs[3]))
+    total = top + jnp.log(sum(jnp.exp(part - top) for part in logs))
+    shift = sum(jnp.exp(logs[i] - total) * stats_ref[i, 16:32, :] for i in range(4))
+    share = jnp.exp(stat_ref[0:16, :] - total)
+    table[...] = jnp.concatenate(
+        [share, shift, total, jnp.zeros((80, 128), jnp.float32)], axis=0
+    ).T
+    query_acc[...] = jnp.zeros_like(query_acc)
+    key_rows[...] = jnp.zeros_like(key_rows)
+
+    def column(kind, block):
+        here = jnp.where(lanes(ROWS) == 16 * kind + block, table[...], 0.0)
+        return jnp.sum(here, axis=1, keepdims=True)
+
+    def columns(kind, step):
+        return jnp.concatenate([column(kind, 2 * step), column(kind, 2 * step + 1)], axis=0)
+
     lane = lanes(CHUNK)
-    qd = query_chunk(q_ref, d_ref)
-    high = shift.astype(jnp.bfloat16).astype(jnp.float32)
-    middle = (shift - high).astype(jnp.bfloat16).astype(jnp.float32)
-    low = shift - high - middle
-    extra = jnp.where(
-        lane == 1, -high, jnp.where(lane == 2, -middle, jnp.where(lane == 3, -low, 0.0))
-    )
-    left = jnp.concatenate([jnp.where(lane < HEAD_DIM, qd, 0.0), extra], axis=1).astype(
-        jnp.bfloat16
-    )
-    dprob = lax.dot_general(left, keys[...], NT, preferred_element_type=jnp.float32)
-    weights = p_ref[...]
-    slope = (weights.astype(jnp.float32) * dprob).astype(jnp.bfloat16)
-    query_grad = jnp.dot(slope, keys[:, 0:128], preferred_element_type=jnp.float32)
-    query_grad = query_grad * (factor * 0.125)
-    attended = o_ref[...] * share
-    for block in range(CHUNK // ROWS):
-        rows = slice(block * ROWS, (block + 1) * ROWS)
-        query_ref[block] = fold_rows(query_grad[rows], False).astype(jnp.bfloat16)
-        out_ref[block] = fold_rows(attended[rows], True).astype(jnp.bfloat16)
-    scaled = (qd * factor * jnp.where(lane < HEAD_DIM, 1.0, 0.125)).T.astype(jnp.bfloat16)
-    value_acc[...] += jnp.dot(scaled[0:64], weights, preferred_element_type=jnp.float32)
-    key_acc[...] += jnp.dot(scaled[64:128], slope, preferred_element_type=jnp.float32)
-
-    @pl.when(step == pl.num_programs(0) - 1)
-    def _():
-        for block in range(BLOCKS):
-            cols = slice(block * ROWS, (block + 1) * ROWS)
-            both = jnp.concatenate([value_acc[:, cols], key_acc[:, cols]], axis=0)
-            grad_ref[block] = both.T.astype(jnp.bfloat16)
+
+    def run(width):
+        value_acc[:, 0:width] = jnp.zeros((HEAD_DIM, width), jnp.float32)
+        key_acc[:, 0:width] = jnp.zeros((HEAD_DIM, width), jnp.float32)
+
+        def chunk(step, _):
+            rows = rows_at(step * CHUNK, CHUNK, CHUNK)
+            qd = qd_ref[rows, :].astype(jnp.float32)
+            shift, total = columns(1, step), columns(2, step)
+            probs = jnp.exp(scores_of(qd, keys[0:width, :]) - total)
+            high = shift.astype(jnp.bfloat16).astype(jnp.float32)
+            middle = (shift - high).astype(jnp.bfloat16).astype(jnp.float32)
+            low = shift - high - middle
+            extra = jnp.where(
+                lane == 1, -high, jnp.where(lane == 2, -middle, jnp.where(lane == 3, -low, 0.0))
+            )
+            left = jnp.concatenate([jnp.where(lane < HEAD_DIM, qd, 0.0), extra], axis=1)
+            dprob = lax.dot_general(
+                left.astype(jnp.bfloat16), keys[0:width, :], NT, preferred_element_type=jnp.float32
+            )
+            slope = (probs * dprob).astype(jnp.bfloat16)
+            query_acc[rows, :] = (
+                jnp.dot(slope, keys[0:width, 0:128], preferred_element_type=jnp.float32) * 0.125
+            )
+            scaled = (qd * jnp.where(lane < HEAD_DIM, 1.0, 0.125)).T.astype(jnp.bfloat16)
+            value_acc[:, 0:width] += jnp.dot(
+                scaled[0:64], probs.astype(jnp.bfloat16), preferred_element_type=jnp.float32
+            )
+            key_acc[:, 0:width] += jnp.dot(
+                scaled[64:128], slope, preferred_element_type=jnp.float32
+            )
+            return 0
+
+        lax.fori_loop(0, (starts[2 * BLOCKS + 1] + CHUNK - 1) // CHUNK, chunk, 0)
+        for at in range(0, width, ROWS):
+            both = jnp.concatenate(
+                [value_acc[:, at : at + ROWS], key_acc[:, at : at + ROWS]], axis=0
+            )
+            key_rows[at : at + ROWS, :] = both.T.astype(jnp.bfloat16)
+
+    by_width(starts[2 * BLOCKS], run)
+    for block in range(BLOCKS):
+        rows = rows_at(starts[block], ROWS, 16)
+        grad_ref[block] = key_rows[rows, :]
+        rows = rows_at(starts[BLOCKS + block], ROWS, 16)
+        query_ref[block] = fold_rows(query_acc[rows, :], False).astype(jnp.bfloat16)
+
+    for step in range(BLOCKS):
+        rows = slice(step * ROWS, (step + 1) * ROWS)
+        query_acc[rows, :] = o_ref[rows, :] * column(0, step)
+    for block in range(BLOCKS):
+        rows = rows_at(starts[BLOCKS + block], ROWS, 16)
+        out_ref[block] = fold_rows(query_acc[rows, :], True).astype(jnp.bfloat16)
+
+
+def whole(shape):
+    return pl.BlockSpec(shape, lambda i: (0,) * len(shape))
 
 
 def attention_forward(query_all, grad_all, key_all):
-    per = CHUNK // ROWS
+    room = SPAN + ROWS
+    outs = [
+        struct((room, 256)),
+        struct((room, 128)),
+        struct((room, 128), jnp.float32),
+        struct((32, 128), jnp.float32),
+    ]
     return pl.pallas_call(
         forward_kernel,
-        grid=(SPAN // CHUNK,),
-        in_specs=[
-            pl.BlockSpec((per, HALF, 128), lambda i: (i, 0, 0)),
-            pl.BlockSpec((per, HALF, 128), lambda i: (i, 0, 0)),
-            pl.BlockSpec((BLOCKS, ROWS, 128), lambda i: (0, 0, 0)),
-        ],
-        out_specs=[
-            pl.BlockSpec((CHUNK, SPAN), lambda i: (i, 0)),
-            pl.BlockSpec((CHUNK, 128), lambda i: (i, 0)),
-            pl.BlockSpec((48, 128), lambda i: (0, 0)),
-        ],
-        out_shape=[
-            struct((SPAN, SPAN)),
-            struct((SPAN, 128), jnp.float32),
-            struct((48, 128), jnp.float32),
-        ],
-        scratch_shapes=[pltpu.VMEM((SPAN, 256), jnp.bfloat16)],
+        grid=(1,),
+        in_specs=[whole(a.shape) for a in (query_all, grad_all, key_all)],
+        out_specs=[whole(out.shape) for out in outs] + [pl.BlockSpec(memory_space=pltpu.SMEM)],
+        out_shape=outs + [struct((2 * BLOCKS + 2,), jnp.int32)],
         compiler_params=pltpu.CompilerParams(vmem_limit_bytes=WHOLE),
     )(query_all, grad_all, key_all)
 
 
-def attention_backward(query_all, grad_all, key_all, weights, attended, stat, stats):
-    per = CHUNK // ROWS
+def attention_backward(starts, keys, qd, attended, stat, stats):
+    room = SPAN + ROWS
+    half = struct((BLOCKS, HALF, 128))
+    outs = [half, half, struct((BLOCKS, ROWS, 128))]
     return pl.pallas_call(
         backward_kernel,
-        grid=(SPAN // CHUNK,),
-        in_specs=[
-            pl.BlockSpec((per, HALF, 128), lambda i: (i, 0, 0)),
-            pl.BlockSpec((per, HALF, 128), lambda i: (i, 0, 0)),
-            pl.BlockSpec((BLOCKS, ROWS, 128), lambda i: (0, 0, 0)),
-            pl.BlockSpec((CHUNK, SPAN), lambda i: (i, 0)),
-            pl.BlockSpec((CHUNK, 128), lambda i: (i, 0)),
-            pl.BlockSpec((48, 128), lambda i: (0, 0)),
-            pl.BlockSpec((4, 32, 128), lambda i: (0, 0, 0)),
-        ],
-        out_specs=[
-            pl.BlockSpec((per, HALF, 128), lambda i: (i, 0, 0)),
-            pl.BlockSpec((per, HALF, 128), lambda i: (i, 0, 0)),
-            pl.BlockSpec((BLOCKS, ROWS, 128), lambda i: (0, 0, 0)),
-        ],
-        out_shape=[
-            struct((BLOCKS, HALF, 128)),
-            struct((BLOCKS, HALF, 128)),
-            struct((BLOCKS, ROWS, 128)),
-        ],
+        grid=(1,),
+        in_specs=[pl.BlockSpec(memory_space=pltpu.SMEM)]
+        + [whole(a.shape) for a in (keys, qd, attended, stat, stats)],
+        out_specs=[whole(out.shape) for out in outs],
+        out_shape=outs,
         scratch_shapes=[
-            pltpu.VMEM((SPAN, 256), jnp.bfloat16),
             pltpu.VMEM((128, 128), jnp.float32),
+            pltpu.VMEM((room, 128), jnp.float32),
             pltpu.VMEM((HEAD_DIM, SPAN), jnp.float32),
             pltpu.VMEM((HEAD_DIM, SPAN), jnp.float32),
+            pltpu.VMEM((room, 128), jnp.bfloat16),
         ],
         compiler_params=pltpu.CompilerParams(vmem_limit_bytes=WHOLE),
-    )(query_all, grad_all, key_all, weights, attended, stat, stats)
+    )(starts, keys, qd, attended, stat, stats)
 
 
 def keep_mask(anchor, counter, row_ids, col_ids):
@@ -387,6 +435,24 @@
     return keep_mask(seed_ref[0], seed_ref[1], row_ids, col_ids)
 
 
+def compaction(tissue_ref):
+    row = tissue_ref[...].astype(jnp.float32)
+    up = lax.broadcasted_iota(jnp.int32, (ROWS, ROWS), 0)
+    over = lax.broadcasted_iota(jnp.int32, (ROWS, ROWS), 1)
+    upper = jnp.where(up <= over, 1.0, 0.0).astype(jnp.bfloat16)
+    wide = jnp.broadcast_to(row, (16, ROWS)).astype(jnp.bfloat16)
+    rank = jnp.dot(wide, upper, preferred_element_type=jnp.float32)[0:1]
+    at = up.astype(jnp.float32)
+    pack = jnp.where((at == rank - 1.0) & (row > 0.0), 1.0, 0.0)
+    return pack, at >= jnp.sum(row, axis=1, keepdims=True)
+
+
+def moved_rows(pack, rows):
+    return jnp.dot(
+        pack.astype(jnp.bfloat16), rows.astype(jnp.bfloat16), preferred_element_type=jnp.float32
+    )
+
+
 def alive_column(tissue_ref):
     row = tissue_ref[...].astype(jnp.float32)
     return jnp.broadcast_to(row, (ROWS, ROWS)).T
@@ -403,7 +469,7 @@
     return tap
 
 
-def depthwise(flipped, field, above, below, taps_ref, bias, alive, padded):
+def depthwise(flipped, field, above, below, taps_ref, bias, padded):
     ctx = lax.axis_index("ctx")
     width = field.shape[1]
     grid_rows = ROWS // GRID_COLS
@@ -428,7 +494,7 @@
                 else:
                     tap = merged_tap(taps_ref, row, col, cols)
                 total = total + tap.reshape(1, 1, 128) * moved[row : row + grid_rows]
-        yield cols, total.reshape(ROWS, 128) * alive
+        yield cols, total.reshape(ROWS, 128)
 
 
 def front_kernel(
@@ -494,15 +560,6 @@
     drop_full[mine] = (upstream * keep * KEEP_SCALE).astype(jnp.bfloat16)
     drops = [copies.to(drop_full.at[mine], drop_full.at[mine], {"head": h}) for h in heads]
 
-    for copy in for_conv:
-        copy.wait()
-    received(halos)
-    for cols, part in depthwise(
-        False, masked[...], above[...], below[...], taps, bias[...], alive, padded
-    ):
-        full[mine, :, cols] = part.astype(jnp.bfloat16)
-    parts = [copies.to(full.at[mine], full.at[mine], {"head": h}) for h in heads]
-
     q_mine, slot, q_peers = query_peers()
     k_mine, _, k_peers = key_peers()
     for copy in for_grad:
@@ -517,6 +574,8 @@
         )
         for i in range(QUADS)
     )
+    pack, dead = compaction(tissue)
+    out_grad = moved_rows(pack, out_grad)
     for j in range(QUADS):
         pair = out_grad[:, 128 * (j // 2) : 128 * (j // 2) + 128]
         grad_part[j] = fold_rows(pair, j % 2 == 0).astype(jnp.bfloat16)
@@ -525,21 +584,32 @@
     ]
     local = [copies.here(grad_part.at[slot], grad_all.at[q_mine])]
 
+    for copy in for_conv:
+        copy.wait()
+    received(halos)
+    for cols, part in depthwise(
+        False, masked[...], above[...], below[...], taps, bias[...].reshape(1, width), padded
+    ):
+        full[mine, :, cols] = (part * alive).astype(jnp.bfloat16)
+    parts = [copies.to(full.at[mine], full.at[mine], {"head": h}) for h in heads]
+
     for copy in for_project:
         copy.wait()
     received(parts)
     local.append(copies.here(full, full_all))
     unit, _ = normalised(full)
+    gain_row = gain[...].reshape(1, QUADS * width)
     sums = [jnp.zeros((rows, w.shape[2]), jnp.float32) for _ in range(3)]
     for i in range(QUADS):
         span = slice(i * width, (i + 1) * width)
-        normed = (unit[i] * gain[:, span]).astype(jnp.bfloat16)
+        normed = (unit[i] * gain_row[:, span]).astype(jnp.bfloat16)
         for k in range(3):
             sums[k] = sums[k] + jnp.dot(normed, w[k, span, :], preferred_element_type=jnp.float32)
     low = lanes(ROWS) < HEAD_DIM
-    dead = alive == 0.0
+    sums = [moved_rows(pack, part) for part in sums]
     for j in range(QUADS):
         q, k, v = (part[:, 128 * (j // 2) : 128 * (j // 2) + 128] for part in sums)
+        q = jnp.where(dead, DEAD, q)
         query_part[j] = fold_rows(q, j % 2 == 0).astype(jnp.bfloat16)
         if j % 2 == 0:
             both = jnp.where(low, v, pltpu.roll(k, 64, 1))
@@ -629,7 +699,9 @@
     alive = alive_column(tissue)
     column = alive[:, 0:1]
     unit, spread = normalised(full)
+    gain_row = gain[...].reshape(1, QUADS * width)
     low = lanes(ROWS) < HEAD_DIM
+    unpack = compaction(tissue)[0].T
 
     def total(ref, slots):
         parts = [ref[s].astype(jnp.float32) for s in slots]
@@ -641,7 +713,7 @@
             packed = total(ref, [8 * (j // 2) + 2 * k + j % 2 for k in range(4)])
             heads_.append(unfold_rows(packed, j % 2 == 0))
         pairs = [jnp.where(low, heads_[2 * p], heads_[2 * p + 1]) for p in range(2)]
-        return jnp.concatenate(pairs, axis=1).astype(jnp.bfloat16)
+        return moved_rows(unpack, jnp.concatenate(pairs, axis=1)).astype(jnp.bfloat16)
 
     for copy in kept:
         copy.wait()
@@ -651,8 +723,8 @@
     keys = [jnp.where(low, pltpu.roll(both[2 * p], 64, 1), both[2 * p + 1]) for p in range(2)]
     grads = [
         queries(query_all),
-        jnp.concatenate(keys, axis=1).astype(jnp.bfloat16),
-        jnp.concatenate(values, axis=1).astype(jnp.bfloat16),
+        moved_rows(unpack, jnp.concatenate(keys, axis=1)).astype(jnp.bfloat16),
+        moved_rows(unpack, jnp.concatenate(values, axis=1)).astype(jnp.bfloat16),
     ]
     plain = jnp.zeros((ROWS, 1), jnp.float32)
     crossed = jnp.zeros((ROWS, 1), jnp.float32)
@@ -663,7 +735,7 @@
             for k in range(3)
         )
         grad_send[i] = part.astype(jnp.bfloat16)
-        scaled = part * gain[:, span]
+        scaled = part * gain_row[:, span]
         plain = plain + jnp.sum(scaled, axis=1, keepdims=True)
         crossed = crossed + jnp.sum(scaled * unit[i], axis=1, keepdims=True)
     lane = lanes(ROWS)
@@ -689,7 +761,7 @@
     own_gain = jnp.zeros((1, width), jnp.float32)
     for i in range(QUADS):
         own_unit = jnp.where(mine == i, unit[i], own_unit)
-        own_gain = jnp.where(mine == i, gain[:, i * width : (i + 1) * width], own_gain)
+        own_gain = jnp.where(mine == i, gain_row[:, i * width : (i + 1) * width], own_gain)
     received(scattered)
     sums = (sums_recv[0] + sums_recv[1]) + (sums_recv[2] + sums_recv[3])
     means = jnp.concatenate([sums, jnp.zeros((120, 128), jnp.float32)], axis=0).T / (QUADS * width)
@@ -705,12 +777,12 @@
     received(branches)
     branch = total(branch_recv, range(QUADS))
     residual = full[mine].astype(jnp.float32)
-    encoded[...] = ((residual + branch * keep * KEEP_SCALE) * column).astype(jnp.bfloat16)
+    encoded[...] = (residual + branch * keep * KEEP_SCALE).astype(jnp.bfloat16)
     outs = [copies.here(encoded, encoded_out)]
 
     received(halos)
     for cols, part in depthwise(
-        True, source[...], above[...], below[...], taps, None, alive, padded
+        True, source[...], above[...], below[...], taps, None, padded
     ):
         result[:, cols] = part.astype(jnp.bfloat16)
     outs.append(copies.here(result, tokens_out))
@@ -740,8 +812,6 @@
 
 def on_device(tokens, tissue, conv_taps, conv_bias, ln_gain, w_qkv, w_out, drop_seed, grad_out):
     rows, width = tokens.shape
-    gain_row = ln_gain[None, :]
-    bias_row = conv_bias[None, :]
     tissue_row = tissue[None, :]
     weights_in = w_qkv.transpose(1, 0, 2)
     half, whole = (HALF, 128), (ROWS, 128)
@@ -767,8 +837,8 @@
             like(tissue_row),
             like(grad_out),
             like(conv_taps),
-            like(bias_row),
-            like(gain_row),
+            like(conv_bias),
+            like(ln_gain),
             like(weights_in),
             like(w_out),
             held((rows, width)),
@@ -788,17 +858,17 @@
         tissue_row,
         grad_out,
         conv_taps,
-        bias_row,
-        gain_row,
+        conv_bias,
+        ln_gain,
         weights_in,
         w_out,
     )
-    weights, attended, stat = attention_forward(query_all, grad_all, key_all)
+    keys, qd, attended, stat, starts = attention_forward(query_all, grad_all, key_all)
     (stats,) = remote_call(
         stat_kernel, 2, [struct((4, 32, 128), jnp.float32)], [], 3, 1, stat
     )
     out_part, query_part, key_part = attention_backward(
-        query_all, grad_all, key_all, weights, attended, stat, stats
+        starts, keys, qd, attended, stat, stats
     )
     encoded, grad_tokens = remote_call(
         back_kernel,
@@ -808,7 +878,7 @@
             like(tissue_row),
             like(grad_out),
             like(conv_taps),
-            like(gain_row),
+            like(ln_gain),
             like(weights_in),
             like(w_out),
             held((QUADS, rows, width)),
@@ -838,11 +908,12 @@
         tissue_row,
         grad_out,
         conv_taps,
-        gain_row,
+        ln_gain,
         weights_in,
         w_out,
     )
-    return (encoded, grad_tokens)
+    alive = tissue.astype(jnp.bfloat16)[:, None]
+    return (encoded * alive, grad_tokens * alive)
 
 
 def solution(mesh):

time: 125 us -> 108 us (0.86)
  Pallas kernels: 118 us -> 106 us
  local copies, waits for them, and re-layouts: 5.63 us -> 0.01 us
  other arithmetic: 0 us -> 1.71 us
    pallas_call x2, Pallas kernels: 28.9 us -> 15 us  [the longest x1 8.65 us: attention_forward(): pl.pallas_call(forward_kernel, grid=(1,), in_specs=[whole(a.shape) for a...]
    unnamed x2, local copies, waits for them, and re-layouts: 3.09 us -> 0.01 us
    broadcast_in_dim x2 -> x0, local copies, waits for them, and re-layouts: 2.54 us -> none  [the longest x1 1.29 us: on_device(): gain_row = ln_gain[None, :]]
    mul x0 -> x1, other arithmetic: none -> 1.71 us  [on_device(): return (encoded * alive, grad_tokens * alive)]
    pallas_call x3, Pallas kernels: 89.3 us -> 90.6 us  [remote_call(): pl.pallas_call(body, out_shape=outs, in_specs=[smem if a.shape == (2,) el...]
where the time goes in v2:
time: 108 us
  Pallas kernels  106 us (98%)
  other arithmetic  1.71 us (2%)
    pallas_call x3, Pallas kernels, remote_call(): pl.pallas_call(body, out_shape=outs, in_specs=[smem if a.shape == (2,) el...  90.6 us
    pallas_call x1, Pallas kernels, attention_forward(): pl.pallas_call(forward_kernel, grid=(1,), in_specs=[whole(a.shape) for a...  8.65 us
    pallas_call x1, Pallas kernels, attention_backward(): pl.pallas_call(backward_kernel, grid=(1,), in_specs=[pl.BlockSpec(memory_...  6.35 us

profile of v2, /device:TPU:1, one launch (start us, length us, event | category | flops | bytes accessed | tf_op | source)
XLA Modules:
  0.0 108.0 jit_solution(4093806524888136266)
XLA Ops:
  0.6 43.6 %shard_map.104 = (bf16[16,64,128]{2,1,0:T(8,128)(2,1)}, bf16[16,64,128]{2,1,0:T(8,128)(2,1)}, bf16[16,128,128]{2,1,0:T(8,128)(2,1)}, bf16[4,128,384]{2,1,0:T(8,128)(2,1)}) custom-call(s32[2]{0:T(128)} %seed_ref.3, bf16[128,384]{1,0:T(8,128)(2,1)} %tokens_in.1, s32[1,128]{1,0:T(1,128)} %bitcast.4, bf16[128,384]{1,0:T(8,128)(2,1)} %grad_in.3, ...), custom_call_target="tpu_custom_call" | custom-call | tf_op jit(solution)/shard_map/pallas_call | solution.py:796
  44.2 8.6 %shard_map.105 = (bf16[2176,256]{1,0:T(8,128)(2,1)}, bf16[2176,128]{1,0:T(8,128)(2,1)}, f32[2176,128]{1,0:T(8,128)}, f32[32,128]{1,0:T(8,128)}, s32[34]{0:T(128)}) custom-call(bf16[16,64,128]{2,1,0:T(8,128)(2,1)} %get-tuple-element.16.q_ref, bf16[16,64,128]{2,1,0:T(8,128)(2,1)} %get-tuple-element.17.d_ref, bf16[16,128,128]{2,1,0:T(8,128)(2,1)} %get-tuple-element.18.vk_ref), custom_call_target="tpu_custom_call" | custom-call | tf_op jit(solution)/shard_map/pallas_call | solution.py:385
  52.9 7.2 %shard_map.106.stats_ref = f32[4,32,128]{2,1,0:T(8,128)} custom-call(f32[32,128]{1,0:T(8,128)} %get-tuple-element.23.stats.stat_ref), custom_call_target="tpu_custom_call" | custom-call | tf_op jit(solution)/shard_map/pallas_call | solution.py:796
  60.1 6.4 %shard_map.107 = (bf16[16,64,128]{2,1,0:T(8,128)(2,1)}, bf16[16,64,128]{2,1,0:T(8,128)(2,1)}, bf16[16,128,128]{2,1,0:T(8,128)(2,1)}) custom-call(s32[34]{0:T(128)} %get-tuple-element.19.starts, bf16[2176,256]{1,0:T(8,128)(2,1)} %get-tuple-element.20.keys, bf16[2176,128]{1,0:T(8,128)(2,1)} %get-tuple-element.21.qd_ref, f32[2176,128]{1,0:T(8,128)} %get-tuple-element.22.o_ref, ...), custom_call_target="tpu_custom_call" | custom-call | tf_op jit(solution)/shard_map/pallas_call | solution.py:399
  66.5 0.0 copy-start
  66.5 39.8 %shard_map.108 = (bf16[128,384]{1,0:T(8,128)(2,1)}, bf16[128,384]{1,0:T(8,128)(2,1)}) custom-call(s32[2]{0:T(128)} %seed_ref.3, bf16[16,64,128]{2,1,0:T(8,128)(2,1)} %get-tuple-element.24.attended_in, bf16[16,64,128]{2,1,0:T(8,128)(2,1)} %get-tuple-element.25.query_in, bf16[16,128,128]{2,1,0:T(8,128)(2,1)} %get-tuple-element.26.key_in, ...), custom_call_target="tpu_custom_call" | custom-call | tf_op jit(solution)/shard_map/pallas_call | solution.py:796
  106.3 0.0 copy-done
  106.3 1.7 %broadcast_multiply_fusion = (bf16[128,384]{1,0:T(8,128)(2,1)}, bf16[128,384]{1,0:T(8,128)(2,1)}) fusion(bf16[128,384]{1,0:T(8,128)(2,1)} %get-tuple-element.29, bf16[128]{0:T(256)(128)(2,1)S(1)} %convert_element_type.3, bf16[128,384]{1,0:T(8,128)(2,1)} %get-tuple-element.28), kind=kLoop, calls=%fused_computation | loop fusion | flops 98304 | bytes 393472 | tf_op jit(solution)/shard_map/mul | solution.py:916
  (1 shorter events, 0.0 us)
Async XLA Ops:
  66.5 39.8 %copy-start = (s32[128]{0:T(128)S(1)}, s32[128]{0:T(128)}, u32[]{:S(2)}) copy-start(s32[128]{0:T(128)} %param.10) | copy-start | bytes 1540

commit v3 on v2

v3 whole, which is shorter than its diff:
```python
import jax
import jax.numpy as jnp
from jax import lax
from jax.experimental import pallas as pl
from jax.experimental.pallas import tpu as pltpu
from jax.sharding import PartitionSpec as P

HEAD_DIM = 64
GRID_COLS = 32
ROWS = 128
QUADS = 4
BLOCKS = 16
SPAN = BLOCKS * ROWS
CHUNK = 256
HALF = ROWS // 2
WHOLE = 60 << 20
CHUNKS = SPAN // CHUNK

DROP_LEVEL = 103
KEEP_SCALE = 1024.0 / 921.0
NEG = -1e30
EPS = 1e-05
DEAD = 2.0**100

MESH = pl.DeviceIdType.MESH
ANY = pl.BlockSpec(memory_space=pl.ANY)
NT = (((1,), (1,)), ((), ()))


def struct(shape, dtype=jnp.bfloat16):
    return jax.ShapeDtypeStruct(shape, dtype)


def div(a, b):
    return lax.div(a, jnp.int32(b))


def mod(a, b):
    return lax.rem(a, jnp.int32(b))


def place():
    ctx = lax.axis_index("ctx")
    return ctx, div(ctx, 16), mod(div(ctx, 8), 2), mod(ctx, 8)


def query_peers():
    ctx, x, y, z = place()
    mine = mod(ctx, 16)
    peers = []
    for step in range(1, 16):
        to = mod(mine + step, 16)
        peers.append((x * 16 + to, to, 2 * div(to, 8) + mod(to, 2)))
    return mine, 2 * y + mod(z, 2), peers


def key_peers():
    ctx, x, y, z = place()
    mine = x * 4 + y * 2 + mod(z, 2)
    base = 2 * div(z, 2)
    peers = []
    for step in range(1, 16):
        to = mod(mine + step, 16)
        peers.append((div(to, 2) * 8 + base + mod(to, 2), to, mod(to, 4)))
    return mine, 2 * y + mod(z, 2), peers


def stat_peers():
    ctx, x, y, z = place()
    mine = div(z, 2)
    base = ctx - z + mod(z, 2)
    peers = []
    for step in range(1, 4):
        to = mod(mine + step, 4)
        peers.append((base + to * 2, to))
    return mine, peers


def head_peers():
    mine = lax.axis_index("head")
    return mine, [mod(mine + step, 4) for step in range(1, 4)]


class Copies:
    def __init__(self, send, recv, own):
        self.send, self.recv, self.own = send, recv, own
        self.far, self.near = [], []

    def to(self, src, dst, device, recv=None):
        at = len(self.far)
        copy = pltpu.make_async_remote_copy(
            src_ref=src,
            dst_ref=dst,
            send_sem=self.send.at[at],
            recv_sem=self.recv.at[at] if recv is None else recv,
            device_id=device,
            device_id_type=MESH,
        )
        copy.start()
        self.far.append(copy)
        return copy

    def here(self, src, dst):
        copy = pltpu.make_async_copy(src, dst, self.own.at[len(self.near)])
        copy.start()
        self.near.append(copy)
        return copy

    def sent(self):
        for copy in self.far:
            copy.wait_send()


def received(copies):
    for copy in copies:
        copy.wait_recv()


def arriving(slot, send, recv, device):
    return pltpu.make_async_remote_copy(
        src_ref=slot,
        dst_ref=slot,
        send_sem=send,
        recv_sem=recv,
        device_id=device,
        device_id_type=MESH,
    )


def ring_ids():
    ctx = lax.axis_index("ctx")
    return mod(ctx + 63, 64), mod(ctx + 1, 64)


def everyone():
    before, after = ring_ids()
    ids = [{"ctx": before}, {"ctx": after}]
    ids += [{"head": h} for h in head_peers()[1]]
    ids += [{"ctx": c} for c, _, _ in query_peers()[2]]
    return ids + [{"ctx": c} for c, _, _ in key_peers()[2]]


def announce(ids):
    barrier = pltpu.get_barrier_semaphore()
    for device in ids:
        pl.semaphore_signal(barrier, inc=1, device_id=device, device_id_type=MESH)


def all_here(ids):
    pl.semaphore_wait(pltpu.get_barrier_semaphore(), len(ids))


def lanes(rows, width=128):
    return lax.broadcasted_iota(jnp.int32, (rows, width), 1)


def normalised(full_ref):
    parts = [full_ref[i].astype(jnp.float32) for i in range(QUADS)]
    width = QUADS * parts[0].shape[1]
    mean = sum(jnp.sum(p, axis=1, keepdims=True) for p in parts) / width
    parts = [p - mean for p in parts]
    var = sum(jnp.sum(p * p, axis=1, keepdims=True) for p in parts) / width
    spread = lax.rsqrt(var + EPS)
    return [p * spread for p in parts], spread


def fold(top, bottom, low_half):
    low = lanes(top.shape[0]) < HEAD_DIM
    if low_half:
        return jnp.where(low, top, pltpu.roll(bottom, 64, 1))
    return jnp.where(low, pltpu.roll(top, 64, 1), bottom)


def fold_rows(block, low_half):
    return fold(block[0:64], block[64:128], low_half)


def unfold_rows(packed, low_half):
    moved = pltpu.roll(packed, 64, 1)
    return jnp.concatenate([packed, moved] if low_half else [moved, packed], axis=0)


def query_chunk(q_ref, d_ref, at):
    blocks = []
    for block in range(CHUNK // ROWS):
        q = unfold_rows(q_ref[2 * at + block].astype(jnp.float32), False)
        d = unfold_rows(d_ref[2 * at + block].astype(jnp.float32), True)
        blocks.append(jnp.where(lanes(ROWS) < HEAD_DIM, d, q))
    return jnp.concatenate(blocks, axis=0)


def key_block(part):
    part = part.astype(jnp.float32)
    alive = part[:, 0:1] < DEAD / 2
    lane = lanes(ROWS)
    extra = jnp.where(lane == 0, jnp.where(alive, 0.0, NEG), jnp.where(lane < 4, 1.0, 0.0))
    return jnp.concatenate([jnp.where(alive, part, 0.0), extra], axis=1).astype(jnp.bfloat16)


def rows_at(start, count_, multiple):
    return pl.ds(pl.multiple_of(start, multiple), count_)


def scores_of(qd, keys):
    lane = lanes(CHUNK)
    left = jnp.concatenate(
        [jnp.where(lane >= HEAD_DIM, qd * 0.125, 0.0), jnp.where(lane == 0, 1.0, 0.0)], axis=1
    ).astype(jnp.bfloat16)
    return lax.dot_general(left, keys, NT, preferred_element_type=jnp.float32)


def forward_chunk(qd, keys, weights, rows, attended):
    lane = lanes(CHUNK)
    scores = scores_of(qd, keys[...])
    highest = jnp.max(scores, axis=1, keepdims=True)
    part = jnp.exp(scores - highest).astype(jnp.bfloat16)
    weights[rows, :] = part
    summed = jnp.dot(part, keys[...], preferred_element_type=jnp.float32)
    totals = summed[:, 129:130]
    mine = summed[:, 0:128] / totals
    attended[rows, :] = mine
    inner = jnp.sum(jnp.where(lane < HEAD_DIM, mine * qd, 0.0), axis=1, keepdims=True)
    log_total = highest + jnp.log(totals)
    table = jnp.where(
        lane == 0, log_total, jnp.where(lane == 1, inner, jnp.where(lane == 2, highest, 0.0))
    ).T
    parts = [table[k : k + 1, h : h + 128] for k in range(3) for h in (0, 128)]
    return jnp.concatenate(parts + [jnp.zeros((2, 128), jnp.float32)], axis=0)


def chunk_columns(stats, mine):
    logs = [stats[i][0:2] for i in range(4)]
    top = jnp.maximum(jnp.maximum(logs[0], logs[1]), jnp.maximum(logs[2], logs[3]))
    total = top + jnp.log(sum(jnp.exp(part - top) for part in logs))
    shift = sum(jnp.exp(logs[i] - total) * stats[i][2:4] for i in range(4))
    share = jnp.exp(mine[0:2] - total)
    factor = jnp.exp(mine[4:6] - total)
    rows = jnp.concatenate([share, shift, factor, jnp.zeros((122, 128), jnp.float32)], axis=0).T
    return [
        jnp.concatenate([rows[:, k : k + 1], rows[:, k + 1 : k + 2]], axis=0) for k in (0, 2, 4)
    ]


def backward_chunk(qd, keys, weights, shift, factor, value_acc, key_acc):
    lane = lanes(CHUNK)
    high = shift.astype(jnp.bfloat16).astype(jnp.float32)
    middle = (shift - high).astype(jnp.bfloat16).astype(jnp.float32)
    low = shift - high - middle
    extra = jnp.where(
        lane == 1, -high, jnp.where(lane == 2, -middle, jnp.where(lane == 3, -low, 0.0))
    )
    left = jnp.concatenate([jnp.where(lane < HEAD_DIM, qd, 0.0), extra], axis=1)
    dprob = lax.dot_general(
        left.astype(jnp.bfloat16), keys[...], NT, preferred_element_type=jnp.float32
    )
    slope = (weights.astype(jnp.float32) * dprob).astype(jnp.bfloat16)
    query_grad = jnp.dot(slope, keys[:, 0:128], preferred_element_type=jnp.float32)
    scaled = (qd * factor * jnp.where(lane < HEAD_DIM, 1.0, 0.125)).T.astype(jnp.bfloat16)
    value_acc[...] += jnp.dot(scaled[0:64], weights, preferred_element_type=jnp.float32)
    key_acc[...] += jnp.dot(scaled[64:128], slope, preferred_element_type=jnp.float32)
    return query_grad * (factor * 0.125)


def keep_mask(anchor, counter, row_ids, col_ids):
    mixed = (
        row_ids * jnp.int32(374761393)
        + col_ids * jnp.int32(668265263)
        + anchor * jnp.int32(1274126177)
        + counter
    )
    mixed = jnp.bitwise_xor(mixed, lax.shift_right_logical(mixed, jnp.full_like(mixed, 15)))
    mixed = mixed * jnp.int32(16777619)
    mixed = jnp.bitwise_xor(mixed, lax.shift_right_logical(mixed, jnp.full_like(mixed, 13)))
    mixed = mixed * jnp.int32(1274126177)
    mixed = jnp.bitwise_xor(mixed, lax.shift_right_logical(mixed, jnp.full_like(mixed, 16)))
    return (jnp.bitwise_and(mixed, jnp.int32(1023)) >= DROP_LEVEL).astype(jnp.float32)


def own_keep(seed_ref, rows, width):
    row_ids = lax.axis_index("ctx") * rows + lax.broadcasted_iota(jnp.int32, (rows, width), 0)
    col_ids = lax.axis_index("head") * width + lax.broadcasted_iota(jnp.int32, (rows, width), 1)
    return keep_mask(seed_ref[0], seed_ref[1], row_ids, col_ids)


def alive_column(tissue_ref):
    row = tissue_ref[...].astype(jnp.float32)
    return jnp.broadcast_to(row, (ROWS, ROWS)).T


def merged_tap(taps_ref, row, col, cols):
    tap = taps_ref[row * 7 + col : row * 7 + col + 1, cols]
    if 1 <= row <= 5 and 1 <= col <= 5:
        at = 49 + (row - 1) * 5 + col - 1
        tap = tap + taps_ref[at : at + 1, cols]
    if 2 <= row <= 4 and 2 <= col <= 4:
        at = 74 + (row - 2) * 3 + col - 2
        tap = tap + taps_ref[at : at + 1, cols]
    return tap


def depthwise(flipped, field, above, below, taps_ref, bias, padded):
    ctx = lax.axis_index("ctx")
    width = field.shape[1]
    grid_rows = ROWS // GRID_COLS
    has_above = jnp.where(ctx > 0, 1.0, 0.0)
    has_below = jnp.where(ctx < 63, 1.0, 0.0)
    field = field.astype(jnp.float32)
    padded[:, 0:8, :] = jnp.zeros((grid_rows + 6, 8, width), jnp.float32)
    padded[:, 40:48, :] = jnp.zeros((grid_rows + 6, 8, width), jnp.float32)
    padded[0:3, 8:40, :] = (above.astype(jnp.float32) * has_above).reshape(3, GRID_COLS, width)
    padded[3:7, 8:40, :] = field.reshape(grid_rows, GRID_COLS, width)
    padded[7:10, 8:40, :] = (below.astype(jnp.float32) * has_below).reshape(3, GRID_COLS, width)
    for start in range(0, width, 128):
        cols = slice(start, start + 128)
        total = field[:, cols].reshape(grid_rows, GRID_COLS, 128)
        if bias is not None:
            total = total + bias[:, cols].reshape(1, 1, 128)
        for col in range(7):
            moved = padded[:, 5 + col : 37 + col, cols]
            for row in range(7):
                if flipped:
                    tap = merged_tap(taps_ref, 6 - row, 6 - col, cols)
                else:
                    tap = merged_tap(taps_ref, row, col, cols)
                total = total + tap.reshape(1, 1, 128) * moved[row : row + grid_rows]
        yield cols, total.reshape(ROWS, 128)


def block_kernel(
    seed_ref,
    tokens_in,
    tissue_in,
    grad_in,
    taps_in,
    bias_in,
    gain_in,
    w_in,
    w_out_in,
    encoded_out,
    tokens_out,
    tokens,
    tissue,
    grad,
    taps,
    bias,
    gain,
    w,
    w_out,
    keep,
    masked,
    above,
    below,
    above_back,
    below_back,
    drop_full,
    full,
    query_part,
    grad_part,
    key_part,
    query_all,
    grad_all,
    key_all,
    keys,
    weights,
    attended,
    stats,
    value_acc,
    key_acc,
    query_out,
    out_out,
    key_out,
    query_back,
    out_back,
    key_back,
    grad_send,
    grad_recv,
    branch_send,
    branch_recv,
    sums_send,
    sums_recv,
    source,
    encoded,
    result,
    padded,
    send,
    recv,
    own,
    query_recv,
    grad_sem,
    key_recv,
    stat_send,
    stat_recv,
    query_back_send,
    query_back_recv,
    out_back_send,
    out_back_recv,
    key_back_recv,
):
    rows, width = tokens.shape
    ids = everyone()
    announce(ids)
    copies = Copies(send, recv, own)
    first = [
        copies.here(src, dst)
        for src, dst in ((tokens_in, tokens), (tissue_in, tissue), (grad_in, grad))
    ]
    for_conv = [copies.here(taps_in, taps), copies.here(bias_in, bias)]
    for_grad = [copies.here(w_out_in, w_out)]
    for_project = [copies.here(gain_in, gain), copies.here(w_in, w)]
    before, after = ring_ids()
    mine, heads = head_peers()
    q_mine, slot, q_peers = query_peers()
    k_mine, _, k_peers = key_peers()
    s_mine, s_peers = stat_peers()
    query_base = lax.axis_index("ctx") - q_mine
    keep[...] = own_keep(seed_ref, rows, width)
    for copy in first:
        copy.wait()
    alive = alive_column(tissue)
    column = alive[:, 0:1]
    masked[...] = (tokens[...].astype(jnp.float32) * column).astype(jnp.bfloat16)
    all_here(ids)
    halos = [
        copies.to(masked.at[pl.ds(32, 96)], above, {"ctx": after}),
        copies.to(masked.at[pl.ds(0, 96)], below, {"ctx": before}),
    ]
    upstream = grad[...].astype(jnp.float32) * column
    drop_full[mine] = (upstream * keep[...] * KEEP_SCALE).astype(jnp.bfloat16)
    drops = [copies.to(drop_full.at[mine], drop_full.at[mine], {"head": h}) for h in heads]

    for copy in for_grad:
        copy.wait()
    received(drops)
    out_grad = sum(
        lax.dot_general(
            drop_full[i],
            w_out[:, i * width : (i + 1) * width],
            NT,
            preferred_element_type=jnp.float32,
        )
        for i in range(QUADS)
    )
    for j in range(QUADS):
        pair = out_grad[:, 128 * (j // 2) : 128 * (j // 2) + 128]
        grad_part[j] = fold_rows(pair, j % 2 == 0).astype(jnp.bfloat16)
    for c, _, h in q_peers:
        copies.to(grad_part.at[h], grad_all.at[q_mine], {"ctx": c}, grad_sem.at[q_mine])
    grad_all[q_mine] = grad_part[slot]

    for copy in for_conv:
        copy.wait()
    received(halos)
    for cols, part in depthwise(
        False, masked[...], above[...], below[...], taps, bias[...].reshape(1, width), padded
    ):
        full[mine, :, cols] = (part * alive).astype(jnp.bfloat16)
    parts = [copies.to(full.at[mine], full.at[mine], {"head": h}) for h in heads]
    for copy in for_project:
        copy.wait()
    received(parts)
    unit, _ = normalised(full)
    gain_row = gain[...].reshape(1, QUADS * width)
    sums = [jnp.zeros((rows, w.shape[2]), jnp.float32) for _ in range(3)]
    for i in range(QUADS):
        span = slice(i * width, (i + 1) * width)
        normed = (unit[i] * gain_row[:, span]).astype(jnp.bfloat16)
        for k in range(3):
            sums[k] = sums[k] + jnp.dot(normed, w[k, span, :], preferred_element_type=jnp.float32)
    low = lanes(ROWS) < HEAD_DIM
    dead = alive == 0.0
    for j in range(QUADS):
        q, k, v = (part[:, 128 * (j // 2) : 128 * (j // 2) + 128] for part in sums)
        query_part[j] = fold_rows(q, j % 2 == 0).astype(jnp.bfloat16)
        if j % 2 == 0:
            both = jnp.where(low, v, pltpu.roll(k, 64, 1))
        else:
            both = jnp.where(low, pltpu.roll(v, 64, 1), k)
        key_part[j] = jnp.where(dead, DEAD, both).astype(jnp.bfloat16)
    for c, _, h in k_peers:
        copies.to(key_part.at[h], key_all.at[k_mine], {"ctx": c}, key_recv.at[k_mine])
    for c, _, h in q_peers:
        copies.to(query_part.at[h], query_all.at[q_mine], {"ctx": c}, query_recv.at[q_mine])
    query_all[q_mine] = query_part[slot]
    keys[rows_at(k_mine * ROWS, ROWS, ROWS), :] = key_block(key_part[slot])
    value_acc[...] = jnp.zeros_like(value_acc)
    key_acc[...] = jnp.zeros_like(key_acc)
    for c, at, _ in k_peers:
        arriving(key_all.at[at], send.at[0], key_recv.at[at], {"ctx": c}).wait_recv()
        keys[rows_at(at * ROWS, ROWS, ROWS), :] = key_block(key_all[at])

    def forward_step(step, _):
        chunk = mod(div(q_mine, 2) + step, CHUNKS)
        for half in range(2):
            at = 2 * chunk + half

            @pl.when(at != q_mine)
            def _(at=at):
                peer = {"ctx": query_base + at}
                arriving(grad_all.at[at], send.at[0], grad_sem.at[at], peer).wait_recv()
                arriving(query_all.at[at], send.at[0], query_recv.at[at], peer).wait_recv()

        qd = query_chunk(query_all, grad_all, chunk)
        rows_ = rows_at(chunk * CHUNK, CHUNK, CHUNK)
        stats[chunk, s_mine] = forward_chunk(qd, keys, weights, rows_, attended)
        for i, (c, _) in enumerate(s_peers):
            pltpu.make_async_remote_copy(
                src_ref=stats.at[chunk, s_mine],
                dst_ref=stats.at[chunk, s_mine],
                send_sem=stat_send.at[chunk, i],
                recv_sem=stat_recv.at[chunk, s_mine],
                device_id={"ctx": c},
                device_id_type=MESH,
            ).start()
        return 0

    lax.fori_loop(0, CHUNKS, forward_step, 0)

    def backward_step(step, _):
        chunk = mod(div(q_mine, 2) + step, CHUNKS)
        for c, at in s_peers:
            arriving(
                stats.at[chunk, at], send.at[0], stat_recv.at[chunk, at], {"ctx": c}
            ).wait_recv()
        share, shift, factor = chunk_columns(
            [stats[chunk, i] for i in range(4)], stats[chunk, s_mine]
        )
        qd = query_chunk(query_all, grad_all, chunk)
        rows_ = rows_at(chunk * CHUNK, CHUNK, CHUNK)
        query_grad = backward_chunk(
            qd, keys, weights[rows_, :], shift, factor, value_acc, key_acc
        )
        out = attended[rows_, :] * share
        for half in range(2):
            at = 2 * chunk + half
            span = slice(half * ROWS, (half + 1) * ROWS)
            query_out[at] = fold_rows(query_grad[span], False).astype(jnp.bfloat16)
            out_out[at] = fold_rows(out[span], True).astype(jnp.bfloat16)

            @pl.when(at != q_mine)
            def _(at=at):
                for src, dst, sent, got in (
                    (query_out, query_back, query_back_send, query_back_recv),
                    (out_out, out_back, out_back_send, out_back_recv),
                ):
                    pltpu.make_async_remote_copy(
                        src_ref=src.at[at],
                        dst_ref=dst.at[q_mine],
                        send_sem=sent.at[at],
                        recv_sem=got.at[q_mine],
                        device_id={"ctx": query_base + at},
                        device_id_type=MESH,
                    ).start()

        return 0

    lax.fori_loop(0, CHUNKS, backward_step, 0)
    for block in range(BLOCKS):
        cols = slice(block * ROWS, (block + 1) * ROWS)
        both = jnp.concatenate([value_acc[:, cols], key_acc[:, cols]], axis=0)
        key_out[block] = both.T.astype(jnp.bfloat16)
    for c, at, _ in k_peers:
        copies.to(key_out.at[at], key_back.at[k_mine], {"ctx": c}, key_back_recv.at[k_mine])
    key_back[k_mine] = key_out[k_mine]
    query_back[q_mine] = query_out[q_mine]
    out_back[q_mine] = out_out[q_mine]

    def total(ref, slots):
        parts = [ref[s].astype(jnp.float32) for s in slots]
        return (parts[0] + parts[1]) + (parts[2] + parts[3])

    def queries(ref):
        heads_ = []
        for j in range(QUADS):
            packed = total(ref, [8 * (j // 2) + 2 * k + j % 2 for k in range(4)])
            heads_.append(unfold_rows(packed, j % 2 == 0))
        pairs = [jnp.where(low, heads_[2 * p], heads_[2 * p + 1]) for p in range(2)]
        return jnp.concatenate(pairs, axis=1).astype(jnp.bfloat16)

    unit, spread = normalised(full)
    for c, at, _ in q_peers:
        arriving(out_back.at[at], send.at[0], out_back_recv.at[at], {"ctx": c}).wait_recv()
    out = queries(out_back)
    for i in range(QUADS):
        span = slice(i * width, (i + 1) * width)
        branch_send[i] = jnp.dot(
            out, w_out[:, span], preferred_element_type=jnp.float32
        ).astype(jnp.bfloat16)
    branches = [copies.to(branch_send.at[h], branch_recv.at[mine], {"head": h}) for h in heads]
    branch_recv[mine] = branch_send[mine]

    for c, at, _ in q_peers:
        arriving(query_back.at[at], send.at[0], query_back_recv.at[at], {"ctx": c}).wait_recv()
    query_sum = queries(query_back)
    for c, at, _ in k_peers:
        arriving(key_back.at[at], send.at[0], key_back_recv.at[at], {"ctx": c}).wait_recv()
    both = [total(key_back, [4 * k + j for k in range(4)]) for j in range(QUADS)]
    value_sum = [jnp.where(low, both[2 * p], pltpu.roll(both[2 * p + 1], 64, 1)) for p in range(2)]
    key_sum = [jnp.where(low, pltpu.roll(both[2 * p], 64, 1), both[2 * p + 1]) for p in range(2)]
    grads = [
        query_sum,
        jnp.concatenate(key_sum, axis=1).astype(jnp.bfloat16),
        jnp.concatenate(value_sum, axis=1).astype(jnp.bfloat16),
    ]
    plain = jnp.zeros((ROWS, 1), jnp.float32)
    crossed = jnp.zeros((ROWS, 1), jnp.float32)
    for i in range(QUADS):
        span = slice(i * width, (i + 1) * width)
        part = sum(
            lax.dot_general(grads[k], w[k, span, :], NT, preferred_element_type=jnp.float32)
            for k in range(3)
        )
        grad_send[i] = part.astype(jnp.bfloat16)
        scaled = part * gain_row[:, span]
        plain = plain + jnp.sum(scaled, axis=1, keepdims=True)
        crossed = crossed + jnp.sum(scaled * unit[i], axis=1, keepdims=True)
    lane = lanes(ROWS)
    sums_send[...] = jnp.where(lane == 0, plain, jnp.where(lane == 1, crossed, 0.0)).T[0:8]
    scattered = []
    for h in heads:
        scattered.append(copies.to(grad_send.at[h], grad_recv.at[mine], {"head": h}))
        scattered.append(copies.to(sums_send, sums_recv.at[mine], {"head": h}))
    grad_recv[mine] = grad_send[mine]
    sums_recv[mine] = sums_send[...]

    received(branches)
    branch = total(branch_recv, range(QUADS))
    residual = full[mine].astype(jnp.float32)
    encoded[...] = (residual + branch * keep[...] * KEEP_SCALE).astype(jnp.bfloat16)
    outs = [copies.here(encoded, encoded_out)]
    own_unit = jnp.zeros((ROWS, width), jnp.float32)
    own_gain = jnp.zeros((1, width), jnp.float32)
    for i in range(QUADS):
        own_unit = jnp.where(mine == i, unit[i], own_unit)
        own_gain = jnp.where(mine == i, gain_row[:, i * width : (i + 1) * width], own_gain)
    received(scattered)
    means = (sums_recv[0] + sums_recv[1]) + (sums_recv[2] + sums_recv[3])
    means = jnp.concatenate([means, jnp.zeros((120, 128), jnp.float32)], axis=0).T / (QUADS * width)
    scaled = total(grad_recv, range(QUADS)) * own_gain
    inner = scaled - means[:, 0:1] - own_unit * means[:, 1:2]
    column = alive_column(tissue)[:, 0:1]
    upstream = grad[...].astype(jnp.float32) * column
    source[...] = ((upstream + inner * spread) * column).astype(jnp.bfloat16)
    halos = [
        copies.to(source.at[pl.ds(32, 96)], above_back, {"ctx": after}),
        copies.to(source.at[pl.ds(0, 96)], below_back, {"ctx": before}),
    ]
    received(halos)
    for cols, part in depthwise(
        True, source[...], above_back[...], below_back[...], taps, None, padded
    ):
        result[:, cols] = part.astype(jnp.bfloat16)
    outs.append(copies.here(result, tokens_out))

    copies.sent()
    for chunk in range(CHUNKS):
        for i, (c, _) in enumerate(s_peers):
            tile = stats.at[chunk, s_mine]
            arriving(tile, stat_send.at[chunk, i], stat_recv.at[chunk, s_mine], {"ctx": c}).wait_send()
    for c, at, _ in q_peers:
        peer = {"ctx": c}
        arriving(query_out.at[at], query_back_send.at[at], query_back_recv.at[at], peer).wait_send()
        arriving(out_out.at[at], out_back_send.at[at], out_back_recv.at[at], peer).wait_send()
    for copy in outs:
        copy.wait()


def on_device(tokens, tissue, conv_taps, conv_bias, ln_gain, w_qkv, w_out, drop_seed, grad_out):
    rows, width = tokens.shape
    args = [
        tokens,
        tissue[None, :],
        grad_out,
        conv_taps,
        conv_bias,
        ln_gain,
        w_qkv.transpose(1, 0, 2),
        w_out,
    ]
    far = 2 + 3 + 15 + 3 + 15 + 15 + 15 + 3 + 6 + 2

    def held(*shape, dtype=jnp.bfloat16):
        return pltpu.VMEM(shape, dtype)

    def sems(*shape):
        return pltpu.SemaphoreType.DMA(shape)

    f32 = jnp.float32
    quads = held(QUADS, rows, width)
    halves = held(BLOCKS, HALF, 128)
    wholes = held(BLOCKS, ROWS, 128)
    halo = held(96, width)
    own = held(rows, width)
    scratch = [pltpu.VMEM(a.shape, a.dtype) for a in args]
    scratch += [held(rows, width, dtype=f32), own, halo, halo, halo, halo, quads, quads]
    scratch += [held(QUADS, HALF, 128), held(QUADS, HALF, 128), held(QUADS, ROWS, 128)]
    scratch += [halves, halves, wholes, held(SPAN, 256), held(SPAN, SPAN)]
    scratch += [held(SPAN, 128, dtype=f32), held(CHUNKS, 4, 8, 128, dtype=f32)]
    scratch += [held(HEAD_DIM, SPAN, dtype=f32), held(HEAD_DIM, SPAN, dtype=f32)]
    scratch += [halves, halves, wholes, halves, halves, wholes]
    scratch += [quads, quads, quads, quads, held(8, rows, dtype=f32), held(QUADS, 8, rows, dtype=f32)]
    scratch += [own, own, own, held(rows // GRID_COLS + 6, 48, width, dtype=f32)]
    scratch += [sems(far), sems(far), sems(10), sems(BLOCKS), sems(BLOCKS), sems(BLOCKS)]
    scratch += [sems(CHUNKS, 3), sems(CHUNKS, 4)] + [sems(BLOCKS)] * 5
    encoded, grad_tokens = pl.pallas_call(
        block_kernel,
        out_shape=[struct((rows, width))] * 2,
        in_specs=[pl.BlockSpec(memory_space=pltpu.SMEM)] + [ANY] * len(args),
        out_specs=[ANY] * 2,
        scratch_shapes=scratch,
        compiler_params=pltpu.CompilerParams(
            collective_id=1, has_side_effects=True, vmem_limit_bytes=WHOLE
        ),
    )(drop_seed, *args)
    alive = tissue.astype(jnp.bfloat16)[:, None]
    return (encoded * alive, grad_tokens * alive)


def solution(mesh):
    placed = (
        P("ctx", "head"),
        P("ctx"),
        P(None, "head"),
        P("head"),
        P(),
        P(None, None, "head"),
        P("head", None),
        P(),
        P("ctx", "head"),
    )
    return jax.shard_map(
        on_device,
        mesh=mesh,
        in_specs=placed,
        out_specs=(P("ctx", "head"), P("ctx", "head")),
        check_vma=False,
    )
```

time: 108 us -> 101 us (0.935)
  Pallas kernels: 106 us -> 97.4 us
    pallas_call x5 -> x1, Pallas kernels: 106 us -> 97.4 us  [on_device(): pl.pallas_call(block_kernel, out_shape=[struct((rows, width))] * 2, in_sp...]
where the time goes in v3:
time: 101 us; the launch traced here: 100 us
  Pallas kernels  97.4 us (96%)
  other arithmetic  2.37 us (2%)
    pallas_call x1, Pallas kernels, on_device(): pl.pallas_call(block_kernel, out_shape=[struct((rows, width))] * 2, in_sp...  97.4 us

profile of v3, /device:TPU:1, one launch (start us, length us, event | category | flops | bytes accessed | tf_op | source)
XLA Modules:
  0.0 100.4 jit_solution(16992539617443449803)
XLA Ops:
  0.6 0.7 convert_element_type.3
  1.3 97.4 %shard_map.104 = (bf16[128,384]{1,0:T(8,128)(2,1)}, bf16[128,384]{1,0:T(8,128)(2,1)}) custom-call(s32[2]{0:T(128)} %seed_ref.1, bf16[128,384]{1,0:T(8,128)(2,1)} %tokens_in.1, s32[1,128]{1,0:T(1,128)} %bitcast.3, bf16[128,384]{1,0:T(8,128)(2,1)} %grad_in.1, f32[83,384]{1,0:T(8,128)} %taps_in.1, f32[384]{0:T(512)} %bias_in.1, f32[1536]{0:T(1024)} %gain_in.1, ...), custom_call_target="tpu_custom_call" | custom-call | tf_op jit(solution)/shard_map/pallas_call | solution.py:704
  98.7 1.7 %broadcast_multiply_fusion = (bf16[128,384]{1,0:T(8,128)(2,1)}, bf16[128,384]{1,0:T(8,128)(2,1)}) fusion(bf16[128,384]{1,0:T(8,128)(2,1)} %get-tuple-element.5, bf16[128]{0:T(256)(128)(2,1)S(1)} %convert_element_type.3, bf16[128,384]{1,0:T(8,128)(2,1)} %get-tuple-element.4), kind=kLoop, calls=%fused_computation | loop fusion | flops 98304 | bytes 393472 | tf_op jit(solution)/shard_map/mul | solution.py:715

commit v4 on v3

--- a/solution.py
+++ b/solution.py
@@ -11,10 +11,12 @@
 QUADS = 4
 BLOCKS = 16
 SPAN = BLOCKS * ROWS
-CHUNK = 256
+CHUNK = 512
 HALF = ROWS // 2
 WHOLE = 60 << 20
 CHUNKS = SPAN // CHUNK
+PER = CHUNK // ROWS
+TILE = (3 * PER + 7) // 8 * 8
 
 DROP_LEVEL = 103
 KEEP_SCALE = 1024.0 / 921.0
@@ -48,21 +50,27 @@
     ctx, x, y, z = place()
     mine = mod(ctx, 16)
     peers = []
-    for step in range(1, 16):
-        to = mod(mine + step, 16)
-        peers.append((x * 16 + to, to, 2 * div(to, 8) + mod(to, 2)))
+    for up, over in ((1, 4), (1, 3), (1, 5), (0, 4), (1, 2), (1, 6), (0, 3), (0, 5)) + (
+        (1, 1), (1, 7), (0, 2), (0, 6), (1, 0), (0, 1), (0, 7)
+    ):
+        to_y, to_z = mod(y + up, 2), mod(z + over, 8)
+        to = to_y * 8 + to_z
+        peers.append((x * 16 + to, to, 2 * to_y + mod(to_z, 2)))
     return mine, 2 * y + mod(z, 2), peers
 
 
 def key_peers():
     ctx, x, y, z = place()
-    mine = x * 4 + y * 2 + mod(z, 2)
-    base = 2 * div(z, 2)
+    bit = mod(z, 2)
+    mine = x * 4 + y * 2 + bit
     peers = []
-    for step in range(1, 16):
-        to = mod(mine + step, 16)
-        peers.append((div(to, 2) * 8 + base + mod(to, 2), to, mod(to, 4)))
-    return mine, 2 * y + mod(z, 2), peers
+    for side, up, over in ((2, 1, 1), (2, 1, 0), (1, 1, 1), (3, 1, 1), (1, 1, 0), (3, 1, 0)) + (
+        (2, 0, 1), (0, 1, 1), (2, 0, 0), (0, 1, 0), (1, 0, 1), (3, 0, 1), (1, 0, 0), (3, 0, 0), (0, 0, 1)
+    ):
+        to_x, to_y, to_bit = mod(x + side, 4), mod(y + up, 2), mod(bit + over, 2)
+        to = to_x * 4 + to_y * 2 + to_bit
+        peers.append((to_x * 16 + to_y * 8 + z - bit + to_bit, to, to_y * 2 + to_bit))
+    return mine, 2 * y + bit, peers
 
 
 def stat_peers():
@@ -133,11 +141,74 @@
 
 
 def everyone():
+    ids = []
+    for (q, _, _), (k, _, _) in zip(query_peers()[2], key_peers()[2]):
+        ids += [{"ctx": q}, {"ctx": k}]
     before, after = ring_ids()
-    ids = [{"ctx": before}, {"ctx": after}]
-    ids += [{"head": h} for h in head_peers()[1]]
-    ids += [{"ctx": c} for c, _, _ in query_peers()[2]]
-    return ids + [{"ctx": c} for c, _, _ in key_peers()[2]]
+    return ids + [{"ctx": before}, {"ctx": after}] + [{"head": h} for h in head_peers()[1]]
+
+
+class Halo:
+    def __init__(self, field, above, below, send, recv):
+        self.ctx = lax.axis_index("ctx")
+        before, after = ring_ids()
+        self.above, self.below = above, below
+        self.down, self.up = [], []
+        for tile in range(field.shape[1] // 128):
+            cols = pl.ds(tile * 128, 128)
+            for side, (rows, dst, to, list_) in enumerate(
+                ((32, above, after, self.down), (0, below, before, self.up))
+            ):
+                list_.append(
+                    pltpu.make_async_remote_copy(
+                        src_ref=field.at[pl.ds(rows, 96), cols],
+                        dst_ref=dst.at[:, cols],
+                        send_sem=send.at[side, tile],
+                        recv_sem=recv.at[side, tile],
+                        device_id={"ctx": to},
+                        device_id_type=MESH,
+                    )
+                )
+
+    def clear(self):
+        @pl.when(self.ctx == 0)
+        def _():
+            self.above[...] = jnp.zeros_like(self.above)
+
+        @pl.when(self.ctx == 63)
+        def _():
+            self.below[...] = jnp.zeros_like(self.below)
+
+    def start(self):
+        @pl.when(self.ctx < 63)
+        def _():
+            for copy in self.down:
+                copy.start()
+
+        @pl.when(self.ctx > 0)
+        def _():
+            for copy in self.up:
+                copy.start()
+
+    def ready(self, tile):
+        @pl.when(self.ctx > 0)
+        def _():
+            self.down[tile].wait_recv()
+
+        @pl.when(self.ctx < 63)
+        def _():
+            self.up[tile].wait_recv()
+
+    def sent(self):
+        @pl.when(self.ctx < 63)
+        def _():
+            for copy in self.down:
+                copy.wait_send()
+
+        @pl.when(self.ctx > 0)
+        def _():
+            for copy in self.up:
+                copy.wait_send()
 
 
 def announce(ids):
@@ -182,9 +253,9 @@
 
 def query_chunk(q_ref, d_ref, at):
     blocks = []
-    for block in range(CHUNK // ROWS):
-        q = unfold_rows(q_ref[2 * at + block].astype(jnp.float32), False)
-        d = unfold_rows(d_ref[2 * at + block].astype(jnp.float32), True)
+    for block in range(PER):
+        q = unfold_rows(q_ref[PER * at + block].astype(jnp.float32), False)
+        d = unfold_rows(d_ref[PER * at + block].astype(jnp.float32), True)
         blocks.append(jnp.where(lanes(ROWS) < HEAD_DIM, d, q))
     return jnp.concatenate(blocks, axis=0)
 
@@ -202,7 +273,7 @@
 
 
 def scores_of(qd, keys):
-    lane = lanes(CHUNK)
+    lane = lanes(qd.shape[0])
     left = jnp.concatenate(
         [jnp.where(lane >= HEAD_DIM, qd * 0.125, 0.0), jnp.where(lane == 0, 1.0, 0.0)], axis=1
     ).astype(jnp.bfloat16)
@@ -224,20 +295,22 @@
     table = jnp.where(
         lane == 0, log_total, jnp.where(lane == 1, inner, jnp.where(lane == 2, highest, 0.0))
     ).T
-    parts = [table[k : k + 1, h : h + 128] for k in range(3) for h in (0, 128)]
-    return jnp.concatenate(parts + [jnp.zeros((2, 128), jnp.float32)], axis=0)
+    parts = [table[k : k + 1, h * ROWS : (h + 1) * ROWS] for k in range(3) for h in range(PER)]
+    return jnp.concatenate(parts + [jnp.zeros((TILE - 3 * PER, 128), jnp.float32)], axis=0)
 
 
 def chunk_columns(stats, mine):
-    logs = [stats[i][0:2] for i in range(4)]
+    logs = [stats[i][0:PER] for i in range(4)]
     top = jnp.maximum(jnp.maximum(logs[0], logs[1]), jnp.maximum(logs[2], logs[3]))
     total = top + jnp.log(sum(jnp.exp(part - top) for part in logs))
-    shift = sum(jnp.exp(logs[i] - total) * stats[i][2:4] for i in range(4))
-    share = jnp.exp(mine[0:2] - total)
-    factor = jnp.exp(mine[4:6] - total)
-    rows = jnp.concatenate([share, shift, factor, jnp.zeros((122, 128), jnp.float32)], axis=0).T
+    shift = sum(jnp.exp(logs[i] - total) * stats[i][PER : 2 * PER] for i in range(4))
+    share = jnp.exp(mine[0:PER] - total)
+    factor = jnp.exp(mine[2 * PER : 3 * PER] - total)
+    rest = jnp.zeros((128 - 3 * PER, 128), jnp.float32)
+    rows = jnp.concatenate([share, shift, factor, rest], axis=0).T
     return [
-        jnp.concatenate([rows[:, k : k + 1], rows[:, k + 1 : k + 2]], axis=0) for k in (0, 2, 4)
+        jnp.concatenate([rows[:, k * PER + h : k * PER + h + 1] for h in range(PER)], axis=0)
+        for k in range(3)
     ]
 
 
@@ -298,23 +371,19 @@
     return tap
 
 
-def depthwise(flipped, field, above, below, taps_ref, bias, padded):
-    ctx = lax.axis_index("ctx")
-    width = field.shape[1]
+def depthwise(flipped, field_ref, halo, taps_ref, bias, padded):
+    width = field_ref.shape[1]
     grid_rows = ROWS // GRID_COLS
-    has_above = jnp.where(ctx > 0, 1.0, 0.0)
-    has_below = jnp.where(ctx < 63, 1.0, 0.0)
-    field = field.astype(jnp.float32)
-    padded[:, 0:8, :] = jnp.zeros((grid_rows + 6, 8, width), jnp.float32)
-    padded[:, 40:48, :] = jnp.zeros((grid_rows + 6, 8, width), jnp.float32)
-    padded[0:3, 8:40, :] = (above.astype(jnp.float32) * has_above).reshape(3, GRID_COLS, width)
-    padded[3:7, 8:40, :] = field.reshape(grid_rows, GRID_COLS, width)
-    padded[7:10, 8:40, :] = (below.astype(jnp.float32) * has_below).reshape(3, GRID_COLS, width)
-    for start in range(0, width, 128):
-        cols = slice(start, start + 128)
-        total = field[:, cols].reshape(grid_rows, GRID_COLS, 128)
+    padded[3:7, 8:40, :] = field_ref[...].astype(jnp.float32).reshape(grid_rows, GRID_COLS, width)
+    for tile in range(width // 128):
+        cols = slice(tile * 128, tile * 128 + 128)
+        total = padded[3:7, 8:40, cols]
         if bias is not None:
             total = total + bias[:, cols].reshape(1, 1, 128)
+        halo.ready(tile)
+        for start, ref in ((0, halo.above), (7, halo.below)):
+            part = ref[:, cols].astype(jnp.float32)
+            padded[start : start + 3, 8:40, cols] = part.reshape(3, GRID_COLS, 128)
         for col in range(7):
             moved = padded[:, 5 + col : 37 + col, cols]
             for row in range(7):
@@ -395,6 +464,10 @@
     out_back_send,
     out_back_recv,
     key_back_recv,
+    halo_send,
+    halo_recv,
+    halo_back_send,
+    halo_back_recv,
 ):
     rows, width = tokens.shape
     ids = everyone()
@@ -407,12 +480,17 @@
     for_conv = [copies.here(taps_in, taps), copies.here(bias_in, bias)]
     for_grad = [copies.here(w_out_in, w_out)]
     for_project = [copies.here(gain_in, gain), copies.here(w_in, w)]
-    before, after = ring_ids()
     mine, heads = head_peers()
     q_mine, slot, q_peers = query_peers()
     k_mine, _, k_peers = key_peers()
     s_mine, s_peers = stat_peers()
     query_base = lax.axis_index("ctx") - q_mine
+    halo = Halo(masked, above, below, halo_send, halo_recv)
+    halo_back = Halo(source, above_back, below_back, halo_back_send, halo_back_recv)
+    halo.clear()
+    halo_back.clear()
+    padded[:, 0:8, :] = jnp.zeros((padded.shape[0], 8, width), jnp.float32)
+    padded[:, 40:48, :] = jnp.zeros((padded.shape[0], 8, width), jnp.float32)
     keep[...] = own_keep(seed_ref, rows, width)
     for copy in first:
         copy.wait()
@@ -420,13 +498,16 @@
     column = alive[:, 0:1]
     masked[...] = (tokens[...].astype(jnp.float32) * column).astype(jnp.bfloat16)
     all_here(ids)
-    halos = [
-        copies.to(masked.at[pl.ds(32, 96)], above, {"ctx": after}),
-        copies.to(masked.at[pl.ds(0, 96)], below, {"ctx": before}),
-    ]
+    halo.start()
     upstream = grad[...].astype(jnp.float32) * column
     drop_full[mine] = (upstream * keep[...] * KEEP_SCALE).astype(jnp.bfloat16)
     drops = [copies.to(drop_full.at[mine], drop_full.at[mine], {"head": h}) for h in heads]
+
+    for copy in for_conv:
+        copy.wait()
+    for cols, part in depthwise(False, masked, halo, taps, bias[...].reshape(1, width), padded):
+        full[mine, :, cols] = (part * alive).astype(jnp.bfloat16)
+    parts = [copies.to(full.at[mine], full.at[mine], {"head": h}) for h in heads]
 
     for copy in for_grad:
         copy.wait()
@@ -447,14 +528,6 @@
         copies.to(grad_part.at[h], grad_all.at[q_mine], {"ctx": c}, grad_sem.at[q_mine])
     grad_all[q_mine] = grad_part[slot]
 
-    for copy in for_conv:
-        copy.wait()
-    received(halos)
-    for cols, part in depthwise(
-        False, masked[...], above[...], below[...], taps, bias[...].reshape(1, width), padded
-    ):
-        full[mine, :, cols] = (part * alive).astype(jnp.bfloat16)
-    parts = [copies.to(full.at[mine], full.at[mine], {"head": h}) for h in heads]
     for copy in for_project:
         copy.wait()
     received(parts)
@@ -488,10 +561,13 @@
         arriving(key_all.at[at], send.at[0], key_recv.at[at], {"ctx": c}).wait_recv()
         keys[rows_at(at * ROWS, ROWS, ROWS), :] = key_block(key_all[at])
 
+    def chunk_at(step):
+        return mod(div(q_mine, PER) + 1 + step, CHUNKS)
+
     def forward_step(step, _):
-        chunk = mod(div(q_mine, 2) + step, CHUNKS)
-        for half in range(2):
-            at = 2 * chunk + half
+        chunk = chunk_at(step)
+        for half in range(PER):
+            at = PER * chunk + half
 
             @pl.when(at != q_mine)
             def _(at=at):
@@ -500,8 +576,9 @@
                 arriving(query_all.at[at], send.at[0], query_recv.at[at], peer).wait_recv()
 
         qd = query_chunk(query_all, grad_all, chunk)
-        rows_ = rows_at(chunk * CHUNK, CHUNK, CHUNK)
-        stats[chunk, s_mine] = forward_chunk(qd, keys, weights, rows_, attended)
+        stats[chunk, s_mine] = forward_chunk(
+            qd, keys, weights, rows_at(chunk * CHUNK, CHUNK, CHUNK), attended
+        )
         for i, (c, _) in enumerate(s_peers):
             pltpu.make_async_remote_copy(
                 src_ref=stats.at[chunk, s_mine],
@@ -516,7 +593,7 @@
     lax.fori_loop(0, CHUNKS, forward_step, 0)
 
     def backward_step(step, _):
-        chunk = mod(div(q_mine, 2) + step, CHUNKS)
+        chunk = chunk_at(step)
         for c, at in s_peers:
             arriving(
                 stats.at[chunk, at], send.at[0], stat_recv.at[chunk, at], {"ctx": c}
@@ -530,8 +607,8 @@
             qd, keys, weights[rows_, :], shift, factor, value_acc, key_acc
         )
         out = attended[rows_, :] * share
-        for half in range(2):
-            at = 2 * chunk + half
+        for half in range(PER):
+            at = PER * chunk + half
             span = slice(half * ROWS, (half + 1) * ROWS)
             query_out[at] = fold_rows(query_grad[span], False).astype(jnp.bfloat16)
             out_out[at] = fold_rows(out[span], True).astype(jnp.bfloat16)
@@ -640,17 +717,13 @@
     column = alive_column(tissue)[:, 0:1]
     upstream = grad[...].astype(jnp.float32) * column
     source[...] = ((upstream + inner * spread) * column).astype(jnp.bfloat16)
-    halos = [
-        copies.to(source.at[pl.ds(32, 96)], above_back, {"ctx": after}),
-        copies.to(source.at[pl.ds(0, 96)], below_back, {"ctx": before}),
-    ]
-    received(halos)
-    for cols, part in depthwise(
-        True, source[...], above_back[...], below_back[...], taps, None, padded
-    ):
+    halo_back.start()
+    for cols, part in depthwise(True, source, halo_back, taps, None, padded):
         result[:, cols] = part.astype(jnp.bfloat16)
     outs.append(copies.here(result, tokens_out))
 
+    halo.sent()
+    halo_back.sent()
     copies.sent()
     for chunk in range(CHUNKS):
         for i, (c, _) in enumerate(s_peers):
@@ -676,7 +749,7 @@
         w_qkv.transpose(1, 0, 2),
         w_out,
     ]
-    far = 2 + 3 + 15 + 3 + 15 + 15 + 15 + 3 + 6 + 2
+    far = 3 + 15 + 3 + 15 + 15 + 15 + 3 + 6
 
     def held(*shape, dtype=jnp.bfloat16):
         return pltpu.VMEM(shape, dtype)
@@ -694,13 +767,14 @@
     scratch += [held(rows, width, dtype=f32), own, halo, halo, halo, halo, quads, quads]
     scratch += [held(QUADS, HALF, 128), held(QUADS, HALF, 128), held(QUADS, ROWS, 128)]
     scratch += [halves, halves, wholes, held(SPAN, 256), held(SPAN, SPAN)]
-    scratch += [held(SPAN, 128, dtype=f32), held(CHUNKS, 4, 8, 128, dtype=f32)]
+    scratch += [held(SPAN, 128, dtype=f32), held(CHUNKS, 4, TILE, 128, dtype=f32)]
     scratch += [held(HEAD_DIM, SPAN, dtype=f32), held(HEAD_DIM, SPAN, dtype=f32)]
     scratch += [halves, halves, wholes, halves, halves, wholes]
     scratch += [quads, quads, quads, quads, held(8, rows, dtype=f32), held(QUADS, 8, rows, dtype=f32)]
     scratch += [own, own, own, held(rows // GRID_COLS + 6, 48, width, dtype=f32)]
     scratch += [sems(far), sems(far), sems(10), sems(BLOCKS), sems(BLOCKS), sems(BLOCKS)]
     scratch += [sems(CHUNKS, 3), sems(CHUNKS, 4)] + [sems(BLOCKS)] * 5
+    scratch += [sems(2, width // 128)] * 4
     encoded, grad_tokens = pl.pallas_call(
         block_kernel,
         out_shape=[struct((rows, width))] * 2,
@@ -711,8 +785,9 @@
             collective_id=1, has_side_effects=True, vmem_limit_bytes=WHOLE
         ),
     )(drop_seed, *args)
-    alive = tissue.astype(jnp.bfloat16)[:, None]
-    return (encoded * alive, grad_tokens * alive)
+    alive = tissue[:, None] > 0
+    nothing = jnp.zeros_like(encoded)
+    return (jnp.where(alive, encoded, nothing), jnp.where(alive, grad_tokens, nothing))
 
 
 def solution(mesh):

time: 101 us -> 93.5 us (0.926)
  the two profiles are of different devices: /device:TPU:1 before, /device:TPU:7 now
where the time goes in v4:
time: 93.5 us; the launch traced here: 93.4 us
  Pallas kernels  90.3 us (97%)
  other arithmetic  2.38 us (3%)
    pallas_call x1, Pallas kernels, on_device(): pl.pallas_call(block_kernel, out_shape=[struct((rows, width))] * 2, in_sp...  90.3 us

profile of v4, /device:TPU:7, one launch (start us, length us, event | category | flops | bytes accessed | tf_op | source)
XLA Modules:
  0.0 93.4 jit_solution(4518530395348983773)
XLA Ops:
  0.6 0.7 broadcast_compare_fusion
  1.3 90.3 %shard_map.104 = (bf16[128,384]{1,0:T(8,128)(2,1)}, bf16[128,384]{1,0:T(8,128)(2,1)}) custom-call(s32[2]{0:T(128)} %seed_ref.1, bf16[128,384]{1,0:T(8,128)(2,1)} %tokens_in.1, s32[1,128]{1,0:T(1,128)} %bitcast.3, bf16[128,384]{1,0:T(8,128)(2,1)} %grad_in.1, f32[83,384]{1,0:T(8,128)} %taps_in.1, f32[384]{0:T(512)} %bias_in.1, f32[1536]{0:T(1024)} %gain_in.1, ...), custom_call_target="tpu_custom_call" | custom-call | tf_op jit(solution)/shard_map/pallas_call | solution.py:778
  91.6 1.7 %broadcast_select_fusion = (bf16[128,384]{1,0:T(8,128)(2,1)}, bf16[128,384]{1,0:T(8,128)(2,1)}) fusion(bf16[128,384]{1,0:T(8,128)(2,1)} %get-tuple-element.5, pred[128]{0:T(512)(128)(4,1)S(1)} %broadcast_compare_fusion, bf16[128,384]{1,0:T(8,128)(2,1)} %get-tuple-element.4), kind=kLoop, calls=%fused_computation | loop fusion | flops 98304 | bytes 393344 | tf_op jit(solution)/shard_map/jit(_where)/select_n | solution.py:790

commit v5 on v4

--- a/solution.py
+++ b/solution.py
@@ -631,13 +631,15 @@
         return 0
 
     lax.fori_loop(0, CHUNKS, backward_step, 0)
-    for block in range(BLOCKS):
-        cols = slice(block * ROWS, (block + 1) * ROWS)
+    def key_rows(at):
+        cols = rows_at(at * ROWS, ROWS, ROWS)
         both = jnp.concatenate([value_acc[:, cols], key_acc[:, cols]], axis=0)
-        key_out[block] = both.T.astype(jnp.bfloat16)
+        return both.T.astype(jnp.bfloat16)
+
     for c, at, _ in k_peers:
+        key_out[at] = key_rows(at)
         copies.to(key_out.at[at], key_back.at[k_mine], {"ctx": c}, key_back_recv.at[k_mine])
-    key_back[k_mine] = key_out[k_mine]
+    key_back[k_mine] = key_rows(k_mine)
     query_back[q_mine] = query_out[q_mine]
     out_back[q_mine] = out_out[q_mine]
 
@@ -699,11 +701,6 @@
     grad_recv[mine] = grad_send[mine]
     sums_recv[mine] = sums_send[...]
 
-    received(branches)
-    branch = total(branch_recv, range(QUADS))
-    residual = full[mine].astype(jnp.float32)
-    encoded[...] = (residual + branch * keep[...] * KEEP_SCALE).astype(jnp.bfloat16)
-    outs = [copies.here(encoded, encoded_out)]
     own_unit = jnp.zeros((ROWS, width), jnp.float32)
     own_gain = jnp.zeros((1, width), jnp.float32)
     for i in range(QUADS):
@@ -718,6 +715,11 @@
     upstream = grad[...].astype(jnp.float32) * column
     source[...] = ((upstream + inner * spread) * column).astype(jnp.bfloat16)
     halo_back.start()
+    received(branches)
+    branch = total(branch_recv, range(QUADS))
+    residual = full[mine].astype(jnp.float32)
+    encoded[...] = (residual + branch * keep[...] * KEEP_SCALE).astype(jnp.bfloat16)
+    outs = [copies.here(encoded, encoded_out)]
     for cols, part in depthwise(True, source, halo_back, taps, None, padded):
         result[:, cols] = part.astype(jnp.bfloat16)
     outs.append(copies.here(result, tokens_out))

time: 93.5 us -> 93.5 us (level)
  no operation moved by 1% of the time
where the time goes in v5:
time: 93.5 us; the launch traced here: 93.4 us
  Pallas kernels  90.3 us (97%)
  other arithmetic  2.38 us (3%)
    pallas_call x1, Pallas kernels, on_device(): pl.pallas_call(block_kernel, out_shape=[struct((rows, width))] * 2, in_sp...  90.3 us

profile of v5, /device:TPU:7, one launch (start us, length us, event | category | flops | bytes accessed | tf_op | source)
XLA Modules:
  0.0 93.4 jit_solution(7048720099056633552)
XLA Ops:
  0.6 0.7 broadcast_compare_fusion
  1.3 90.3 %shard_map.104 = (bf16[128,384]{1,0:T(8,128)(2,1)}, bf16[128,384]{1,0:T(8,128)(2,1)}) custom-call(s32[2]{0:T(128)} %seed_ref.1, bf16[128,384]{1,0:T(8,128)(2,1)} %tokens_in.1, s32[1,128]{1,0:T(1,128)} %bitcast.3, bf16[128,384]{1,0:T(8,128)(2,1)} %grad_in.1, f32[83,384]{1,0:T(8,128)} %taps_in.1, f32[384]{0:T(512)} %bias_in.1, f32[1536]{0:T(1024)} %gain_in.1, ...), custom_call_target="tpu_custom_call" | custom-call | tf_op jit(solution)/shard_map/pallas_call | solution.py:780
  91.6 1.7 %broadcast_select_fusion = (bf16[128,384]{1,0:T(8,128)(2,1)}, bf16[128,384]{1,0:T(8,128)(2,1)}) fusion(bf16[128,384]{1,0:T(8,128)(2,1)} %get-tuple-element.5, pred[128]{0:T(512)(128)(4,1)S(1)} %broadcast_compare_fusion, bf16[128,384]{1,0:T(8,128)(2,1)} %get-tuple-element.4), kind=kLoop, calls=%fused_computation | loop fusion | flops 98304 | bytes 393344 | tf_op jit(solution)/shard_map/jit(_where)/select_n | solution.py:792
